TPU v7x, 32 devices: a whole 2x2x4 slice. The times are simulated.
32 devices in a mesh: shots: 2 (over x), blk: 16 (over z, y, core).
Axes of the slice: x: 2, y: 2, z: 4, core: 2. Of those that a mesh axis runs over, the one named last changes fastest.
Arguments:
- source_prev: float32 [32, 8, 64, 256], P(('shots', 'blk')), parts along dimension 0, may hold values from -8 to 8
- source_cur: float32 [32, 8, 64, 256], P(('shots', 'blk')), parts along dimension 0, may hold values from -8 to 8
- receiver_prev: float32 [32, 8, 64, 256], P(('shots', 'blk')), parts along dimension 0, may hold values from -8 to 8
- receiver_cur: float32 [32, 8, 64, 256], P(('shots', 'blk')), parts along dimension 0, may hold values from -8 to 8
- coef_horiz: float32 [16, 8, 64, 256], P('blk'), may hold values from 0.08 to 0.2
- coef_vert: float32 [16, 8, 64, 256], P('blk'), may hold values from 0.04 to 0.1
- coef_mixed: float32 [16, 8, 64, 256], P('blk'), may hold values from -0.05 to 0.05
- live_depth: int32 [16, 8, 64], P('blk'), may hold values from 1 to 256
- offsets: int32 [9], replicated, may hold values from 0 to 8, each once
- image_in: float32 [9, 32, 8, 64, 256], P(None, ('shots', 'blk')), parts along dimension 1, may hold values from -6 to 6
Outputs:
- image_out: float32 [9, 32, 8, 64, 256], P(None, ('shots', 'blk')), parts along dimension 1
- source_last: float32 [32, 8, 64, 256], P(('shots', 'blk')), parts along dimension 0
- receiver_last: float32 [32, 8, 64, 256], P(('shots', 'blk')), parts along dimension 0
There are 2 independent parts, one for each index of `shots`. A program takes and returns all parts, laid end to end along the dimension named above; an argument that names none is the same for every part. Nothing has to cross between parts.
Inputs may be any that keep to these rules, and one draw needn't show every extreme that they name: offsets holds every value from 0 to 8 once.
All inputs are finite; a program needn't handle non-finite values.
Results may differ from a plain program's by a relative error of at most 0.0003.
Values sent between devices are 32-bit elements; how exact they have to be, the bound alone decides.
A program may use at most 64 MiB of HBM per device.

v0:
```python
import jax
import jax.numpy as jnp
from jax import lax
from jax.sharding import PartitionSpec as P

STEPS = 4
RAD = 4
HMAX = 4
NOFF = 9


second_w = (-205.0 / 72.0, 8.0 / 5.0, -1.0 / 5.0, 8.0 / 315.0, -1.0 / 560.0)
first_w = (4.0 / 5.0, -1.0 / 5.0, 4.0 / 105.0, -1.0 / 280.0)


def from_behind(value, axis, steps):
    count = lax.axis_size(axis)
    first, last = (max(0, -steps), min(count, count - steps))
    return lax.ppermute(value, axis, [(source, source + steps) for source in range(first, last)])


def stencil(padded_xy, coef_horiz, coef_vert, coef_mixed):
    count_x = padded_xy.shape[0] - 8
    count_y = padded_xy.shape[1] - 8
    depth = padded_xy.shape[2]
    padded = jnp.pad(padded_xy, ((0, 0), (0, 0), (4, 4)))

    def take(a, b, c):
        return padded[4 + a : 4 + a + count_x, 4 + b : 4 + b + count_y, 4 + c : 4 + c + depth]

    center = take(0, 0, 0)
    horiz = 2.0 * second_w[0] * center
    vert = second_w[0] * center
    deriv_z = jnp.zeros((count_x + 8, count_y, depth), jnp.float32)
    for k in range(1, 5):
        horiz = horiz + second_w[k] * (
            take(k, 0, 0) + take(-k, 0, 0) + take(0, k, 0) + take(0, -k, 0)
        )
        vert = vert + second_w[k] * (take(0, 0, k) + take(0, 0, -k))
        deriv_z = deriv_z + first_w[k - 1] * (
            padded[:, 4 : 4 + count_y, 4 + k : 4 + k + depth]
            - padded[:, 4 : 4 + count_y, 4 - k : 4 - k + depth]
        )
    mixed = jnp.zeros((count_x, count_y, depth), jnp.float32)
    for k in range(1, 5):
        mixed = mixed + first_w[k - 1] * (
            deriv_z[4 + k : 4 + k + count_x] - deriv_z[4 - k : 4 - k + count_x]
        )
    return coef_horiz * horiz + coef_vert * vert + coef_mixed * mixed


def image_terms(src_pad, rec_pad, width, offsets, mute):
    count = mute.shape[0]
    terms = []
    for slot in range(NOFF):
        shift = offsets[slot] - HMAX
        left = lax.dynamic_slice_in_dim(src_pad, width - shift, count, 0)
        right = lax.dynamic_slice_in_dim(rec_pad, width + shift, count, 0)
        terms.append(mute * left * right)
    return jnp.stack(terms)


def wave_rims(field, xdim):
    ydim = xdim + 1
    size_x = field.shape[xdim]
    from_below = from_behind(lax.slice_in_dim(field, size_x - RAD, size_x, axis=xdim), "blk", 1)
    from_above = from_behind(lax.slice_in_dim(field, 0, RAD, axis=xdim), "blk", -1)
    joined = jnp.concatenate([from_below, field, from_above], xdim)
    widths = [(0, 0)] * field.ndim
    widths[ydim] = (RAD, RAD)
    return jnp.pad(joined, widths)


def snap_rims(snaps):
    size_x = snaps.shape[1]
    from_below = from_behind(snaps[:, size_x - HMAX :], "blk", 1)
    from_above = from_behind(snaps[:, :HMAX], "blk", -1)
    return jnp.concatenate([from_below, snaps, from_above], 1)


def wave_pads(source_cur, receiver_cur):
    return (wave_rims(source_cur, 0), wave_rims(receiver_cur, 0))


def per_device(
    source_prev,
    source_cur,
    receiver_prev,
    receiver_cur,
    coef_horiz,
    coef_vert,
    coef_mixed,
    live_depth,
    offsets,
    image_in,
):
    source_prev = source_prev[0]
    source_cur = source_cur[0]
    receiver_prev = receiver_prev[0]
    receiver_cur = receiver_cur[0]
    coef_horiz = coef_horiz[0]
    coef_vert = coef_vert[0]
    coef_mixed = coef_mixed[0]
    span_y = source_cur.shape[1]
    depth_ids = lax.broadcasted_iota(jnp.int32, source_cur.shape, 2)
    mute = (depth_ids < live_depth[0][:, :, None]).astype(jnp.float32)
    image = image_in[:, 0]
    half_steps = STEPS // 2
    for step in range(STEPS):
        src_pad, rec_pad = wave_pads(source_cur, receiver_cur)
        if step > 0 and step % half_steps == 0:
            image = image + image_terms(
                src_pad[:, RAD : RAD + span_y], rec_pad[:, RAD : RAD + span_y], RAD, offsets, mute
            )
        src_new = (
            2.0 * source_cur - source_prev + stencil(src_pad, coef_horiz, coef_vert, coef_mixed)
        )
        rec_new = (
            2.0 * receiver_cur - receiver_prev + stencil(rec_pad, coef_horiz, coef_vert, coef_mixed)
        )
        source_prev, source_cur = (source_cur, src_new)
        receiver_prev, receiver_cur = (receiver_cur, rec_new)
        if (step + 1) % half_steps == 0:
            if step + 1 == STEPS:
                snap_pad = snap_rims(jnp.stack([source_cur, receiver_cur]))
                image = image + image_terms(snap_pad[0], snap_pad[1], HMAX, offsets, mute)
    return (image[:, None], source_cur[None], receiver_cur[None])


def solution(mesh):
    in_specs = (
        P(("shots", "blk"), None, None, None),
        P(("shots", "blk"), None, None, None),
        P(("shots", "blk"), None, None, None),
        P(("shots", "blk"), None, None, None),
        P("blk", None, None, None),
        P("blk", None, None, None),
        P("blk", None, None, None),
        P("blk", None, None),
        P(),
        P(None, ("shots", "blk"), None, None, None),
    )
    out_specs = (
        P(None, ("shots", "blk"), None, None, None),
        P(("shots", "blk"), None, None, None),
        P(("shots", "blk"), None, None, None),
    )
    return jax.shard_map(
        per_device, mesh=mesh, in_specs=in_specs, out_specs=out_specs, check_vma=False
    )
```

profile of v0, /device:TPU:9, one launch (start us, length us, event | category | flops | bytes accessed | tf_op | source)
XLA Modules:
  0.0 127.1 jit_solution(8926772650504436230)
XLA Ops:
  0.7 1.2 slice_bitcast_fusion.1
  1.8 2.6 %collective-permute-start.6 = (f32[4,64,256]{2,1,0:T(8,128)S(1)}, f32[4,64,256]{2,1,0:T(8,128)S(1)}, u32[]{:S(2)}, u32[]{:S(2)}) collective-permute-start(f32[4,64,256]{2,1,0:T(8,128)S(1)} %get-tuple-element.21), channel_id=1, source_target_pairs={{1,0},{2,1},{3,2},{4,3},{5,4},{6,5},{7,6},{8,7},{9,8},{10,9},{11,1... | collective-permute-start | bytes 786440 | tf_op jit(solution)/shard_map/ppermute | solution.py:19
  4.4 3.0 %collective-permute-start.7 = (f32[4,64,256]{2,1,0:T(8,128)S(1)}, f32[4,64,256]{2,1,0:T(8,128)S(1)}, u32[]{:S(2)}, u32[]{:S(2)}) collective-permute-start(f32[4,64,256]{2,1,0:T(8,128)S(1)} %get-tuple-element.22), channel_id=1, source_target_pairs={{0,1},{1,2},{2,3},{3,4},{4,5},{5,6},{6,7},{7,8},{8,9},{9,10},{10,1... | collective-permute-start | bytes 786440 | tf_op jit(solution)/shard_map/ppermute | solution.py:19
  7.5 1.9 %collective-permute-start = (f32[4,64,256]{2,1,0:T(8,128)S(1)}, f32[4,64,256]{2,1,0:T(8,128)S(1)}, u32[]{:S(2)}, u32[]{:S(2)}) collective-permute-start(f32[4,64,256]{2,1,0:T(8,128)S(1)} %get-tuple-element.13), channel_id=1, source_target_pairs={{1,0},{2,1},{3,2},{4,3},{5,4},{6,5},{7,6},{8,7},{9,8},{10,9},{11,1... | collective-permute-start | bytes 786440 | tf_op jit(solution)/shard_map/ppermute | solution.py:19
  9.4 3.6 %collective-permute-start.1 = (f32[4,64,256]{2,1,0:T(8,128)S(1)}, f32[4,64,256]{2,1,0:T(8,128)S(1)}, u32[]{:S(2)}, u32[]{:S(2)}) collective-permute-start(f32[4,64,256]{2,1,0:T(8,128)S(1)} %get-tuple-element.14), channel_id=1, source_target_pairs={{0,1},{1,2},{2,3},{3,4},{4,5},{5,6},{6,7},{7,8},{8,9},{9,10},{10,1... | collective-permute-start | bytes 786440 | tf_op jit(solution)/shard_map/ppermute | solution.py:19
  13.1 0.1 select_maximum_fusion.6
  13.3 2.3 %fusion.27 = f32[16,64,256]{2,1,0:T(8,128)S(1)} fusion(f32[16,72,256]{2,1,0:T(8,128)S(1)} %select_maximum_fusion.6), kind=kLoop, calls=%fused_computation.219 | loop fusion | flops 2883584 | bytes 2228224 | tf_op jit(solution)/shard_map/add | solution.py:40
  15.6 1.8 %fusion.231 = f32[8,64,256]{2,1,0:T(8,128)S(1)} fusion(f32[8,64,256]{2,1,0:T(8,128)S(1)} %bitcast.98, f32[4,64,256]{2,1,0:T(8,128)S(1)} %collective-permute-done.7, f32[4,64,256]{2,1,0:T(8,128)S(1)} %collective-permute-done.6, f32[16,72,256]{2,1,0:T(8,128)S(1)} %select_maximum_fusion.6, f32[16,64,256]{2,1,0:T(8,128)S(1)} %fusion.27, ...), kind=kLoop, calls=%fused_computation.475 | loop fusion | flops 7995392 | bytes 13238272 | tf_op jit(solution)/shard_map/add | solution.py:119
  17.4 2.7 %collective-permute-start.8 = (f32[4,64,256]{2,1,0:T(8,128)S(1)}, f32[4,64,256]{2,1,0:T(8,128)S(1)}, u32[]{:S(2)}, u32[]{:S(2)}) collective-permute-start(f32[4,64,256]{2,1,0:T(8,128)S(1)} %get-tuple-element.19), channel_id=1, source_target_pairs={{1,0},{2,1},{3,2},{4,3},{5,4},{6,5},{7,6},{8,7},{9,8},{10,9},{11,1... | collective-permute-start | bytes 786440 | tf_op jit(solution)/shard_map/ppermute | solution.py:19
  20.2 3.0 %collective-permute-start.9 = (f32[4,64,256]{2,1,0:T(8,128)S(1)}, f32[4,64,256]{2,1,0:T(8,128)S(1)}, u32[]{:S(2)}, u32[]{:S(2)}) collective-permute-start(f32[4,64,256]{2,1,0:T(8,128)S(1)} %get-tuple-element.20), channel_id=1, source_target_pairs={{0,1},{1,2},{2,3},{3,4},{4,5},{5,6},{6,7},{7,8},{8,9},{9,10},{10,1... | collective-permute-start | bytes 786440 | tf_op jit(solution)/shard_map/ppermute | solution.py:19
  23.2 0.1 select_maximum_fusion.10
  23.4 2.3 %fusion.5 = f32[16,64,256]{2,1,0:T(8,128)S(1)} fusion(f32[16,72,256]{2,1,0:T(8,128)S(1)} %select_maximum_fusion.10), kind=kLoop, calls=%fused_computation.197 | loop fusion | flops 2883584 | bytes 2228224 | tf_op jit(solution)/shard_map/add | solution.py:40
  25.7 1.8 %fusion.283 = f32[8,64,256]{2,1,0:T(8,128)S(1)} fusion(f32[8,64,256]{2,1,0:T(8,128)S(1)} %bitcast.100, f32[4,64,256]{2,1,0:T(8,128)S(1)} %collective-permute-done.1, f32[4,64,256]{2,1,0:T(8,128)S(1)} %collective-permute-done, f32[16,72,256]{2,1,0:T(8,128)S(1)} %select_maximum_fusion.10, f32[16,64,256]{2,1,0:T(8,128)S(1)} %fusion.5, ...), kind=kLoop, calls=%fused_computation.527 | loop fusion | flops 7995392 | bytes 13238272 | tf_op jit(solution)/shard_map/add | solution.py:116
  27.5 3.3 %collective-permute-start.2 = (f32[4,64,256]{2,1,0:T(8,128)S(1)}, f32[4,64,256]{2,1,0:T(8,128)S(1)}, u32[]{:S(2)}, u32[]{:S(2)}) collective-permute-start(f32[4,64,256]{2,1,0:T(8,128)S(1)} %get-tuple-element.11), channel_id=1, source_target_pairs={{1,0},{2,1},{3,2},{4,3},{5,4},{6,5},{7,6},{8,7},{9,8},{10,9},{11,1... | collective-permute-start | bytes 786440 | tf_op jit(solution)/shard_map/ppermute | solution.py:19
  30.7 2.3 %collective-permute-start.3 = (f32[4,64,256]{2,1,0:T(8,128)S(1)}, f32[4,64,256]{2,1,0:T(8,128)S(1)}, u32[]{:S(2)}, u32[]{:S(2)}) collective-permute-start(f32[4,64,256]{2,1,0:T(8,128)S(1)} %get-tuple-element.12), channel_id=1, source_target_pairs={{0,1},{1,2},{2,3},{3,4},{4,5},{5,6},{6,7},{7,8},{8,9},{9,10},{10,1... | collective-permute-start | bytes 786440 | tf_op jit(solution)/shard_map/ppermute | solution.py:19
  33.1 0.1 select_maximum_fusion.4
  33.2 2.3 %fusion.38 = f32[16,64,256]{2,1,0:T(8,128)S(1)} fusion(f32[16,72,256]{2,1,0:T(8,128)S(1)} %select_maximum_fusion.4), kind=kLoop, calls=%fused_computation.230 | loop fusion | flops 2883584 | bytes 2228224 | tf_op jit(solution)/shard_map/add | solution.py:40
  35.5 1.8 %fusion.205 = f32[8,64,256]{2,1,0:T(8,128)S(1)} fusion(f32[8,64,256]{2,1,0:T(8,128)S(1)} %fusion.231, f32[4,64,256]{2,1,0:T(8,128)S(1)} %collective-permute-done.9, f32[4,64,256]{2,1,0:T(8,128)S(1)} %collective-permute-done.8, f32[16,72,256]{2,1,0:T(8,128)S(1)} %select_maximum_fusion.4, f32[16,64,256]{2,1,0:T(8,128)S(1)} %fusion.38, ...), kind=kLoop, calls=%fused_computation.449 | loop fusion | flops 7995392 | bytes 13238272 | tf_op jit(solution)/shard_map/add | solution.py:119
  37.3 4.3 %collective-permute-start.10 = (f32[4,64,256]{2,1,0:T(8,128)S(1)}, f32[4,64,256]{2,1,0:T(8,128)S(1)}, u32[]{:S(2)}, u32[]{:S(2)}) collective-permute-start(f32[4,64,256]{2,1,0:T(8,128)S(1)} %get-tuple-element.18), channel_id=1, source_target_pairs={{0,1},{1,2},{2,3},{3,4},{4,5},{5,6},{6,7},{7,8},{8,9},{9,10},{10,1... | collective-permute-start | bytes 786440 | tf_op jit(solution)/shard_map/ppermute | solution.py:19
  41.6 2.1 %collective-permute-start.11 = (f32[4,64,256]{2,1,0:T(8,128)S(1)}, f32[4,64,256]{2,1,0:T(8,128)S(1)}, u32[]{:S(2)}, u32[]{:S(2)}) collective-permute-start(f32[4,64,256]{2,1,0:T(8,128)S(1)} %get-tuple-element.17), channel_id=1, source_target_pairs={{1,0},{2,1},{3,2},{4,3},{5,4},{6,5},{7,6},{8,7},{9,8},{10,9},{11,1... | collective-permute-start | bytes 786440 | tf_op jit(solution)/shard_map/ppermute | solution.py:19
  43.7 0.1 select_maximum_fusion.8
  43.9 2.3 %fusion.16 = f32[16,64,256]{2,1,0:T(8,128)S(1)} fusion(f32[16,72,256]{2,1,0:T(8,128)S(1)} %select_maximum_fusion.8), kind=kLoop, calls=%fused_computation.208 | loop fusion | flops 2883584 | bytes 2228224 | tf_op jit(solution)/shard_map/add | solution.py:40
  46.1 1.8 %fusion.257 = f32[8,64,256]{2,1,0:T(8,128)S(1)} fusion(f32[8,64,256]{2,1,0:T(8,128)S(1)} %fusion.283, f32[4,64,256]{2,1,0:T(8,128)S(1)} %collective-permute-done.3, f32[4,64,256]{2,1,0:T(8,128)S(1)} %collective-permute-done.2, f32[16,72,256]{2,1,0:T(8,128)S(1)} %select_maximum_fusion.8, f32[16,64,256]{2,1,0:T(8,128)S(1)} %fusion.16, ...), kind=kLoop, calls=%fused_computation.501 | loop fusion | flops 7995392 | bytes 13238272 | tf_op jit(solution)/shard_map/add | solution.py:116
  48.0 4.5 %collective-permute-start.4 = (f32[4,64,256]{2,1,0:T(8,128)S(1)}, f32[4,64,256]{2,1,0:T(8,128)S(1)}, u32[]{:S(2)}, u32[]{:S(2)}) collective-permute-start(f32[4,64,256]{2,1,0:T(8,128)S(1)} %get-tuple-element.10), channel_id=1, source_target_pairs={{0,1},{1,2},{2,3},{3,4},{4,5},{5,6},{6,7},{7,8},{8,9},{9,10},{10,1... | collective-permute-start | bytes 786440 | tf_op jit(solution)/shard_map/ppermute | solution.py:19
  52.5 1.9 %collective-permute-start.5 = (f32[4,64,256]{2,1,0:T(8,128)S(1)}, f32[4,64,256]{2,1,0:T(8,128)S(1)}, u32[]{:S(2)}, u32[]{:S(2)}) collective-permute-start(f32[4,64,256]{2,1,0:T(8,128)S(1)} %get-tuple-element.9), channel_id=1, source_target_pairs={{1,0},{2,1},{3,2},{4,3},{5,4},{6,5},{7,6},{8,7},{9,8},{10,9},{11,1... | collective-permute-start | bytes 786440 | tf_op jit(solution)/shard_map/ppermute | solution.py:19
  54.5 0.1 pad_maximum_fusion.2
  54.6 0.1 pad.62
  54.7 2.3 %fusion.71 = f32[16,64,256]{2,1,0:T(8,128)S(1)} fusion(f32[16,72,256]{2,1,0:T(8,128)S(1)} %pad.62), kind=kLoop, calls=%fused_computation.263 | loop fusion | flops 2883584 | bytes 2228224 | tf_op jit(solution)/shard_map/add | solution.py:40
  56.9 1.8 %fusion.126 = f32[8,64,256]{2,1,0:T(8,128)S(1)} fusion(f32[8,64,256]{2,1,0:T(8,128)S(1)} %fusion.205, f32[4,64,256]{2,1,0:T(8,128)S(1)} %collective-permute-done.10, f32[4,64,256]{2,1,0:T(8,128)S(1)} %collective-permute-done.11, f32[16,72,256]{2,1,0:T(8,128)S(1)} %pad.62, f32[16,64,256]{2,1,0:T(8,128)S(1)} %fusion.71, f32[1,8,64,256]{3,2,1,0:T(8,128)S(1)} %copy-done, ...), kind=kLoop, calls=%fused_computation.370 | loop fusion | flops 7995392 | bytes 13238272 | tf_op jit(solution)/shard_map/add | solution.py:119
  58.8 4.4 %collective-permute-start.14 = (f32[4,64,256]{2,1,0:T(8,128)S(1)}, f32[4,64,256]{2,1,0:T(8,128)S(1)}, u32[]{:S(2)}, u32[]{:S(2)}) collective-permute-start(f32[4,64,256]{2,1,0:T(8,128)S(1)} %get-tuple-element.15), channel_id=1, source_target_pairs={{1,0},{2,1},{3,2},{4,3},{5,4},{6,5},{7,6},{8,7},{9,8},{10,9},{11,1... | collective-permute-start | bytes 786440 | tf_op jit(solution)/shard_map/ppermute | solution.py:19
  63.2 1.9 %collective-permute-start.15 = (f32[4,64,256]{2,1,0:T(8,128)S(1)}, f32[4,64,256]{2,1,0:T(8,128)S(1)}, u32[]{:S(2)}, u32[]{:S(2)}) collective-permute-start(f32[4,64,256]{2,1,0:T(8,128)S(1)} %get-tuple-element.16), channel_id=1, source_target_pairs={{0,1},{1,2},{2,3},{3,4},{4,5},{5,6},{6,7},{7,8},{8,9},{9,10},{10,1... | collective-permute-start | bytes 786440 | tf_op jit(solution)/shard_map/ppermute | solution.py:19
  65.1 0.1 pad_maximum_fusion.1
  65.2 0.1 pad.58
  65.4 2.3 %fusion.49 = f32[16,64,256]{2,1,0:T(8,128)S(1)} fusion(f32[16,72,256]{2,1,0:T(8,128)S(1)} %pad.58), kind=kLoop, calls=%fused_computation.241 | loop fusion | flops 2883584 | bytes 2228224 | tf_op jit(solution)/shard_map/add | solution.py:40
  67.6 1.8 %fusion.179 = f32[8,64,256]{2,1,0:T(8,128)S(1)} fusion(f32[8,64,256]{2,1,0:T(8,128)S(1)} %fusion.257, f32[4,64,256]{2,1,0:T(8,128)S(1)} %collective-permute-done.4, f32[4,64,256]{2,1,0:T(8,128)S(1)} %collective-permute-done.5, f32[16,72,256]{2,1,0:T(8,128)S(1)} %pad.58, f32[16,64,256]{2,1,0:T(8,128)S(1)} %fusion.49, f32[1,8,64,256]{3,2,1,0:T(8,128)S(1)} %copy-done, ...), kind=kLoop, calls=%fused_computation.423 | loop fusion | flops 7995392 | bytes 13238272 | tf_op jit(solution)/shard_map/add | solution.py:116
  69.5 2.4 %collective-permute-start.12 = (f32[4,64,256]{2,1,0:T(8,128)S(1)}, f32[4,64,256]{2,1,0:T(8,128)S(1)}, u32[]{:S(2)}, u32[]{:S(2)}) collective-permute-start(f32[4,64,256]{2,1,0:T(8,128)S(1)} %get-tuple-element.7), channel_id=1, source_target_pairs={{1,0},{2,1},{3,2},{4,3},{5,4},{6,5},{7,6},{8,7},{9,8},{10,9},{11,1... | collective-permute-start | bytes 786440 | tf_op jit(solution)/shard_map/ppermute | solution.py:19
  71.9 3.4 %collective-permute-start.13 = (f32[4,64,256]{2,1,0:T(8,128)S(1)}, f32[4,64,256]{2,1,0:T(8,128)S(1)}, u32[]{:S(2)}, u32[]{:S(2)}) collective-permute-start(f32[4,64,256]{2,1,0:T(8,128)S(1)} %get-tuple-element.8), channel_id=1, source_target_pairs={{0,1},{1,2},{2,3},{3,4},{4,5},{5,6},{6,7},{7,8},{8,9},{9,10},{10,1... | collective-permute-start | bytes 786440 | tf_op jit(solution)/shard_map/ppermute | solution.py:19
  75.3 0.1 select_maximum_fusion
  75.4 2.3 %fusion.82 = f32[16,64,256]{2,1,0:T(8,128)S(1)} fusion(f32[16,72,256]{2,1,0:T(8,128)S(1)} %select_maximum_fusion), kind=kLoop, calls=%fused_computation.274 | loop fusion | flops 2883584 | bytes 2228224 | tf_op jit(solution)/shard_map/add | solution.py:40
  77.7 3.4 %collective-permute-done.13 = f32[4,64,256]{2,1,0:T(8,128)S(1)} collective-permute-done((f32[4,64,256]{2,1,0:T(8,128)S(1)}, f32[4,64,256]{2,1,0:T(8,128)S(1)}, u32[]{:S(2)}, u32[]{:S(2)}) %collective-permute-start.13) | collective-permute-done | bytes 262176 | tf_op jit(solution)/shard_map/ppermute | solution.py:19
  81.1 0.1 select_maximum_fusion.2
  81.3 2.3 %fusion.60 = f32[16,64,256]{2,1,0:T(8,128)S(1)} fusion(f32[16,72,256]{2,1,0:T(8,128)S(1)} %select_maximum_fusion.2), kind=kLoop, calls=%fused_computation.252 | loop fusion | flops 2883584 | bytes 2228224 | tf_op jit(solution)/shard_map/add | solution.py:40
  83.6 1.8 %fusion.100 = f32[1,8,64,256]{3,2,1,0:T(8,128)S(1)} fusion(f32[8,64,256]{2,1,0:T(8,128)S(1)} %fusion.126, f32[4,64,256]{2,1,0:T(8,128)S(1)} %collective-permute-done.15, f32[4,64,256]{2,1,0:T(8,128)S(1)} %collective-permute-done.14, f32[16,72,256]{2,1,0:T(8,128)S(1)} %select_maximum_fusion, f32[16,64,256]{2,1,0:T(8,128)S(1)} %fusion.82, ...), kind=kLoop, calls=%fused_computation.344 | loop fusion | flops 7995392 | bytes 13238272 | tf_op jit(solution)/shard_map/stack | solution.py:125
  85.3 1.8 %fusion.153 = f32[1,8,64,256]{3,2,1,0:T(8,128)S(1)} fusion(f32[8,64,256]{2,1,0:T(8,128)S(1)} %fusion.179, f32[4,64,256]{2,1,0:T(8,128)S(1)} %collective-permute-done.13, f32[4,64,256]{2,1,0:T(8,128)S(1)} %collective-permute-done.12, f32[16,72,256]{2,1,0:T(8,128)S(1)} %select_maximum_fusion.2, f32[16,64,256]{2,1,0:T(8,128)S(1)} %fusion.60, ...), kind=kLoop, calls=%fused_computation.397 | loop fusion | flops 7995392 | bytes 13238272 | tf_op jit(solution)/shard_map/stack | solution.py:125
  87.2 1.1 fusion.299
  88.3 4.4 %collective-permute-start.16 = (f32[2,4,64,256]{3,2,1,0:T(8,128)}, f32[2,4,64,256]{3,2,1,0:T(8,128)}, u32[]{:S(2)}, u32[]{:S(2)}) collective-permute-start(f32[2,4,64,256]{3,2,1,0:T(8,128)} %get-tuple-element.5), channel_id=1, source_target_pairs={{0,1},{1,2},{2,3},{3,4},{4,5},{5,6},{6,7},{7,8},{8,9},{9,10},{10,1... | collective-permute-start | bytes 1572872 | tf_op jit(solution)/shard_map/ppermute | solution.py:19
  92.6 1.9 %collective-permute-start.17 = (f32[2,4,64,256]{3,2,1,0:T(8,128)}, f32[2,4,64,256]{3,2,1,0:T(8,128)}, u32[]{:S(2)}, u32[]{:S(2)}) collective-permute-start(f32[2,4,64,256]{3,2,1,0:T(8,128)} %get-tuple-element.6), channel_id=1, source_target_pairs={{1,0},{2,1},{3,2},{4,3},{5,4},{6,5},{7,6},{8,7},{9,8},{10,9},{11,1... | collective-permute-start | bytes 1572872 | tf_op jit(solution)/shard_map/ppermute | solution.py:19
  94.6 0.7 fusion.495
  118.0 0.1 bitcast_dynamic-update-slice_fusion.17
  118.2 1.4 %pad_maximum_fusion = f32[2,16,64,256]{3,2,1,0:T(8,128)S(1)} fusion(f32[2,4,64,256]{3,2,1,0:T(8,128)} %collective-permute-done.17, f32[1,8,64,256]{3,2,1,0:T(8,128)S(1)} %fusion.100, f32[1,8,64,256]{3,2,1,0:T(8,128)S(1)} %fusion.153, f32[2,4,64,256]{3,2,1,0:T(8,128)} %collective-permute-done.16), kind=kLoop, calls=%fused_computation.129 | loop fusion | flops 1572864 | bytes 4194304 | tf_op jit(solution)/shard_map/concatenate | solution.py:78
  119.6 0.1 fusion.488
  119.8 0.2 bitcast_dynamic-update-slice_fusion.16
  120.0 0.2 bitcast_dynamic-update-slice_fusion.15
  120.3 0.2 bitcast_dynamic-update-slice_fusion.14
  120.5 0.2 bitcast_dynamic-update-slice_fusion.13
  120.7 0.2 bitcast_dynamic-update-slice_fusion.12
  121.0 0.2 bitcast_dynamic-update-slice_fusion.11
  121.2 0.0 slice-start.1
  121.2 0.2 bitcast_dynamic-update-slice_fusion.10
  121.5 0.2 bitcast_dynamic-update-slice_fusion.9
  121.7 0.1 bitcast_dynamic-update-slice_fusion
  121.9 1.3 %slice-done = s8[4194304]{0:T(1024)(128)(4,1)S(1)} async-done(((s8[4718592]{0:T(1024)(128)(4,1)}), s8[4194304]{0:T(1024)(128)(4,1)S(1)}, s32[]{:S(2)}) %slice-start) | async-done | bytes 4194328
  123.2 0.2 slice-done.1
  123.3 3.7 %add_add_fusion = f32[9,1,8,64,256]{4,3,2,1,0:T(8,128)} fusion(f32[9,1,8,64,256]{4,3,2,1,0:T(8,128)S(1)} %bitcast_dynamic-update-slice_fusion, f32[9,1,8,64,256]{4,3,2,1,0:T(8,128)S(1)} %bitcast.102, f32[9,1,8,64,256]{4,3,2,1,0:T(8,128)S(1)} %get-tuple-element.23), kind=kLoop, calls=%fused_computation | loop fusion | flops 2359296 | bytes 18874368 | tf_op jit(solution)/shard_map/add | solution.py:126
  (48 shorter events, 0.4 us)
Async XLA Ops:
  0.6 12.5 %copy-start.3 = (f32[1,8,64,256]{3,2,1,0:T(8,128)S(1)}, f32[1,8,64,256]{3,2,1,0:T(8,128)}, u32[]{:S(2)}) copy-start(f32[1,8,64,256]{3,2,1,0:T(8,128)} %param.13) | copy-start | bytes 1572868
  0.6 6.8 %copy-start.4 = (f32[1,8,64,256]{3,2,1,0:T(8,128)S(1)}, f32[1,8,64,256]{3,2,1,0:T(8,128)}, u32[]{:S(2)}) copy-start(f32[1,8,64,256]{3,2,1,0:T(8,128)} %param.11) | copy-start | bytes 1572868
  1.8 11.3 %collective-permute-start.6 = (f32[4,64,256]{2,1,0:T(8,128)S(1)}, f32[4,64,256]{2,1,0:T(8,128)S(1)}, u32[]{:S(2)}, u32[]{:S(2)}) collective-permute-start(f32[4,64,256]{2,1,0:T(8,128)S(1)} %get-tuple-element.21), channel_id=1, source_target_pairs={{1,0},{2,1},{3,2},{4,3},{5,4},{6,5},{7,6},{8,7},{9,8},{10,9},{11,1... | collective-permute-start | bytes 786440 | tf_op jit(solution)/shard_map/ppermute | solution.py:19
  4.4 8.7 %collective-permute-start.7 = (f32[4,64,256]{2,1,0:T(8,128)S(1)}, f32[4,64,256]{2,1,0:T(8,128)S(1)}, u32[]{:S(2)}, u32[]{:S(2)}) collective-permute-start(f32[4,64,256]{2,1,0:T(8,128)S(1)} %get-tuple-element.22), channel_id=1, source_target_pairs={{0,1},{1,2},{2,3},{3,4},{4,5},{5,6},{6,7},{7,8},{8,9},{9,10},{10,1... | collective-permute-start | bytes 786440 | tf_op jit(solution)/shard_map/ppermute | solution.py:19
  7.5 15.7 %collective-permute-start = (f32[4,64,256]{2,1,0:T(8,128)S(1)}, f32[4,64,256]{2,1,0:T(8,128)S(1)}, u32[]{:S(2)}, u32[]{:S(2)}) collective-permute-start(f32[4,64,256]{2,1,0:T(8,128)S(1)} %get-tuple-element.13), channel_id=1, source_target_pairs={{1,0},{2,1},{3,2},{4,3},{5,4},{6,5},{7,6},{8,7},{9,8},{10,9},{11,1... | collective-permute-start | bytes 786440 | tf_op jit(solution)/shard_map/ppermute | solution.py:19
  9.4 13.8 %collective-permute-start.1 = (f32[4,64,256]{2,1,0:T(8,128)S(1)}, f32[4,64,256]{2,1,0:T(8,128)S(1)}, u32[]{:S(2)}, u32[]{:S(2)}) collective-permute-start(f32[4,64,256]{2,1,0:T(8,128)S(1)} %get-tuple-element.14), channel_id=1, source_target_pairs={{0,1},{1,2},{2,3},{3,4},{4,5},{5,6},{6,7},{7,8},{8,9},{9,10},{10,1... | collective-permute-start | bytes 786440 | tf_op jit(solution)/shard_map/ppermute | solution.py:19
  13.3 2.3 %copy-start = (f32[1,8,64,256]{3,2,1,0:T(8,128)S(1)}, f32[1,8,64,256]{3,2,1,0:T(8,128)}, u32[]{:S(2)}) copy-start(f32[1,8,64,256]{3,2,1,0:T(8,128)} %param.16) | copy-start | bytes 1572868
  13.3 2.3 %copy-start.1 = (f32[1,8,64,256]{3,2,1,0:T(8,128)S(1)}, f32[1,8,64,256]{3,2,1,0:T(8,128)}, u32[]{:S(2)}) copy-start(f32[1,8,64,256]{3,2,1,0:T(8,128)} %param.15) | copy-start | bytes 1572868
  13.3 2.3 %copy-start.2 = (f32[1,8,64,256]{3,2,1,0:T(8,128)S(1)}, f32[1,8,64,256]{3,2,1,0:T(8,128)}, u32[]{:S(2)}) copy-start(f32[1,8,64,256]{3,2,1,0:T(8,128)} %param.14) | copy-start | bytes 1572868
  13.3 2.3 %copy-start.8 = (f32[1,8,64,256]{3,2,1,0:T(8,128)S(1)}, f32[1,8,64,256]{3,2,1,0:T(8,128)}, u32[]{:S(2)}) copy-start(f32[1,8,64,256]{3,2,1,0:T(8,128)} %param.12) | copy-start | bytes 1572868
  17.4 15.6 %collective-permute-start.8 = (f32[4,64,256]{2,1,0:T(8,128)S(1)}, f32[4,64,256]{2,1,0:T(8,128)S(1)}, u32[]{:S(2)}, u32[]{:S(2)}) collective-permute-start(f32[4,64,256]{2,1,0:T(8,128)S(1)} %get-tuple-element.19), channel_id=1, source_target_pairs={{1,0},{2,1},{3,2},{4,3},{5,4},{6,5},{7,6},{8,7},{9,8},{10,9},{11,1... | collective-permute-start | bytes 786440 | tf_op jit(solution)/shard_map/ppermute | solution.py:19
  20.2 12.9 %collective-permute-start.9 = (f32[4,64,256]{2,1,0:T(8,128)S(1)}, f32[4,64,256]{2,1,0:T(8,128)S(1)}, u32[]{:S(2)}, u32[]{:S(2)}) collective-permute-start(f32[4,64,256]{2,1,0:T(8,128)S(1)} %get-tuple-element.20), channel_id=1, source_target_pairs={{0,1},{1,2},{2,3},{3,4},{4,5},{5,6},{6,7},{7,8},{8,9},{9,10},{10,1... | collective-permute-start | bytes 786440 | tf_op jit(solution)/shard_map/ppermute | solution.py:19
  23.4 2.3 %copy-start.9 = (f32[1,8,64,256]{3,2,1,0:T(8,128)S(1)}, f32[1,8,64,256]{3,2,1,0:T(8,128)}, u32[]{:S(2)}) copy-start(f32[1,8,64,256]{3,2,1,0:T(8,128)} %param.10) | copy-start | bytes 1572868
  27.5 16.2 %collective-permute-start.2 = (f32[4,64,256]{2,1,0:T(8,128)S(1)}, f32[4,64,256]{2,1,0:T(8,128)S(1)}, u32[]{:S(2)}, u32[]{:S(2)}) collective-permute-start(f32[4,64,256]{2,1,0:T(8,128)S(1)} %get-tuple-element.11), channel_id=1, source_target_pairs={{1,0},{2,1},{3,2},{4,3},{5,4},{6,5},{7,6},{8,7},{9,8},{10,9},{11,1... | collective-permute-start | bytes 786440 | tf_op jit(solution)/shard_map/ppermute | solution.py:19
  30.7 13.0 %collective-permute-start.3 = (f32[4,64,256]{2,1,0:T(8,128)S(1)}, f32[4,64,256]{2,1,0:T(8,128)S(1)}, u32[]{:S(2)}, u32[]{:S(2)}) collective-permute-start(f32[4,64,256]{2,1,0:T(8,128)S(1)} %get-tuple-element.12), channel_id=1, source_target_pairs={{0,1},{1,2},{2,3},{3,4},{4,5},{5,6},{6,7},{7,8},{8,9},{9,10},{10,1... | collective-permute-start | bytes 786440 | tf_op jit(solution)/shard_map/ppermute | solution.py:19
  37.3 17.1 %collective-permute-start.10 = (f32[4,64,256]{2,1,0:T(8,128)S(1)}, f32[4,64,256]{2,1,0:T(8,128)S(1)}, u32[]{:S(2)}, u32[]{:S(2)}) collective-permute-start(f32[4,64,256]{2,1,0:T(8,128)S(1)} %get-tuple-element.18), channel_id=1, source_target_pairs={{0,1},{1,2},{2,3},{3,4},{4,5},{5,6},{6,7},{7,8},{8,9},{9,10},{10,1... | collective-permute-start | bytes 786440 | tf_op jit(solution)/shard_map/ppermute | solution.py:19
  41.6 12.9 %collective-permute-start.11 = (f32[4,64,256]{2,1,0:T(8,128)S(1)}, f32[4,64,256]{2,1,0:T(8,128)S(1)}, u32[]{:S(2)}, u32[]{:S(2)}) collective-permute-start(f32[4,64,256]{2,1,0:T(8,128)S(1)} %get-tuple-element.17), channel_id=1, source_target_pairs={{1,0},{2,1},{3,2},{4,3},{5,4},{6,5},{7,6},{8,7},{9,8},{10,9},{11,1... | collective-permute-start | bytes 786440 | tf_op jit(solution)/shard_map/ppermute | solution.py:19
  48.0 17.2 %collective-permute-start.4 = (f32[4,64,256]{2,1,0:T(8,128)S(1)}, f32[4,64,256]{2,1,0:T(8,128)S(1)}, u32[]{:S(2)}, u32[]{:S(2)}) collective-permute-start(f32[4,64,256]{2,1,0:T(8,128)S(1)} %get-tuple-element.10), channel_id=1, source_target_pairs={{0,1},{1,2},{2,3},{3,4},{4,5},{5,6},{6,7},{7,8},{8,9},{9,10},{10,1... | collective-permute-start | bytes 786440 | tf_op jit(solution)/shard_map/ppermute | solution.py:19
  52.5 12.6 %collective-permute-start.5 = (f32[4,64,256]{2,1,0:T(8,128)S(1)}, f32[4,64,256]{2,1,0:T(8,128)S(1)}, u32[]{:S(2)}, u32[]{:S(2)}) collective-permute-start(f32[4,64,256]{2,1,0:T(8,128)S(1)} %get-tuple-element.9), channel_id=1, source_target_pairs={{1,0},{2,1},{3,2},{4,3},{5,4},{6,5},{7,6},{8,7},{9,8},{10,9},{11,1... | collective-permute-start | bytes 786440 | tf_op jit(solution)/shard_map/ppermute | solution.py:19
  58.8 16.5 %collective-permute-start.14 = (f32[4,64,256]{2,1,0:T(8,128)S(1)}, f32[4,64,256]{2,1,0:T(8,128)S(1)}, u32[]{:S(2)}, u32[]{:S(2)}) collective-permute-start(f32[4,64,256]{2,1,0:T(8,128)S(1)} %get-tuple-element.15), channel_id=1, source_target_pairs={{1,0},{2,1},{3,2},{4,3},{5,4},{6,5},{7,6},{8,7},{9,8},{10,9},{11,1... | collective-permute-start | bytes 786440 | tf_op jit(solution)/shard_map/ppermute | solution.py:19
  63.2 12.1 %collective-permute-start.15 = (f32[4,64,256]{2,1,0:T(8,128)S(1)}, f32[4,64,256]{2,1,0:T(8,128)S(1)}, u32[]{:S(2)}, u32[]{:S(2)}) collective-permute-start(f32[4,64,256]{2,1,0:T(8,128)S(1)} %get-tuple-element.16), channel_id=1, source_target_pairs={{0,1},{1,2},{2,3},{3,4},{4,5},{5,6},{6,7},{7,8},{8,9},{9,10},{10,1... | collective-permute-start | bytes 786440 | tf_op jit(solution)/shard_map/ppermute | solution.py:19
  69.5 8.2 %collective-permute-start.12 = (f32[4,64,256]{2,1,0:T(8,128)S(1)}, f32[4,64,256]{2,1,0:T(8,128)S(1)}, u32[]{:S(2)}, u32[]{:S(2)}) collective-permute-start(f32[4,64,256]{2,1,0:T(8,128)S(1)} %get-tuple-element.7), channel_id=1, source_target_pairs={{1,0},{2,1},{3,2},{4,3},{5,4},{6,5},{7,6},{8,7},{9,8},{10,9},{11,1... | collective-permute-start | bytes 786440 | tf_op jit(solution)/shard_map/ppermute | solution.py:19
  71.9 9.3 %collective-permute-start.13 = (f32[4,64,256]{2,1,0:T(8,128)S(1)}, f32[4,64,256]{2,1,0:T(8,128)S(1)}, u32[]{:S(2)}, u32[]{:S(2)}) collective-permute-start(f32[4,64,256]{2,1,0:T(8,128)S(1)} %get-tuple-element.8), channel_id=1, source_target_pairs={{0,1},{1,2},{2,3},{3,4},{4,5},{5,6},{6,7},{7,8},{8,9},{9,10},{10,1... | collective-permute-start | bytes 786440 | tf_op jit(solution)/shard_map/ppermute | solution.py:19
  85.3 32.9 %copy-start.5 = (f32[1,8,64,256]{3,2,1,0:T(8,128)}, f32[1,8,64,256]{3,2,1,0:T(8,128)S(1)}, u32[]{:S(2)}) copy-start(f32[1,8,64,256]{3,2,1,0:T(8,128)S(1)} %fusion.100) | copy-start | bytes 1572868
  87.1 31.1 %copy-start.6 = (f32[1,8,64,256]{3,2,1,0:T(8,128)}, f32[1,8,64,256]{3,2,1,0:T(8,128)S(1)}, u32[]{:S(2)}) copy-start(f32[1,8,64,256]{3,2,1,0:T(8,128)S(1)} %fusion.153) | copy-start | bytes 1572868
  87.1 7.5 %copy-start.10 = (s32[9]{0:T(128)S(1)}, s32[9]{0:T(128)}, u32[]{:S(2)}) copy-start(s32[9]{0:T(128)} %param.18) | copy-start | bytes 112
  87.1 30.9 %copy-start.7 = (s32[1,8,64]{2,1,0:T(8,128)S(1)}, s32[1,8,64]{2,1,0:T(8,128)}, u32[]{:S(2)}) copy-start(s32[1,8,64]{2,1,0:T(8,128)} %param.17) | copy-start | bytes 6148
  88.3 29.9 %collective-permute-start.16 = (f32[2,4,64,256]{3,2,1,0:T(8,128)}, f32[2,4,64,256]{3,2,1,0:T(8,128)}, u32[]{:S(2)}, u32[]{:S(2)}) collective-permute-start(f32[2,4,64,256]{3,2,1,0:T(8,128)} %get-tuple-element.5), channel_id=1, source_target_pairs={{0,1},{1,2},{2,3},{3,4},{4,5},{5,6},{6,7},{7,8},{8,9},{9,10},{10,1... | collective-permute-start | bytes 1572872 | tf_op jit(solution)/shard_map/ppermute | solution.py:19
  92.6 25.5 %collective-permute-start.17 = (f32[2,4,64,256]{3,2,1,0:T(8,128)}, f32[2,4,64,256]{3,2,1,0:T(8,128)}, u32[]{:S(2)}, u32[]{:S(2)}) collective-permute-start(f32[2,4,64,256]{3,2,1,0:T(8,128)} %get-tuple-element.6), channel_id=1, source_target_pairs={{1,0},{2,1},{3,2},{4,3},{5,4},{6,5},{7,6},{8,7},{9,8},{10,9},{11,1... | collective-permute-start | bytes 1572872 | tf_op jit(solution)/shard_map/ppermute | solution.py:19
  121.0 2.2 %slice-start = ((s8[4718592]{0:T(1024)(128)(4,1)}), s8[4194304]{0:T(1024)(128)(4,1)S(1)}, s32[]{:S(2)}) async-start(s8[4718592]{0:T(1024)(128)(4,1)} %bitcast.101), calls=%async_computation | async-start | bytes 8388608
  121.2 2.1 %slice-start.1 = ((s8[4718592]{0:T(1024)(128)(4,1)}), s8[524288]{0:T(1024)(128)(4,1)S(1)}, s32[]{:S(2)}) async-start(s8[4718592]{0:T(1024)(128)(4,1)} %bitcast.101), calls=%async_computation.1 | async-start | bytes 1048576
where the time goes:
time: 129 us; the launch traced here: 127 us
  starting transfers between devices  53.7 us (42%)
  other arithmetic  41.7 us (32%)
  between operations  24.2 us (19%)
  local copies, waits for them, and re-layouts  3.98 us (3%)
  waiting for transfers between devices  3.47 us (3%)
    ppermute x18, starting transfers between devices, from_behind(): lax.ppermute(value, axis, [(source, source + steps) for source in range(f...  53.7 us
    add x8, other arithmetic, stencil(): deriv_z + first_w[k - 1] * (padded[:, 4:4 + count_y, 4 + k:4 + k + depth]...  18.2 us
    add x3, other arithmetic, per_device(): 2.0 * receiver_cur - receiver_prev  5.29 us
    add x3, other arithmetic, per_device(): 2.0 * source_cur - source_prev  5.29 us
    another operation x3, other arithmetic, per_device(): snap_pad = snap_rims(jnp.stack([source_cur, receiver_cur]))  4.64 us
    add x1, other arithmetic, per_device(): image = image + image_terms(snap_pad[0], snap_pad[1], HMAX, offsets, mute)  3.71 us
    ppermute x18, waiting for transfers between devices, from_behind(): lax.ppermute(value, axis, [(source, source + steps) for source in range(f...  3.47 us
  transfers between devices with their start and end apart: 18, of which 1 were waited for; matrix products, arithmetic and copies ran while one was open for 23% of the time, Pallas kernels for 0%

commit v1 on v0

v1 whole, which is shorter than its diff:
```python
import functools

import jax
import jax.numpy as jnp
import ml_dtypes
import numpy as np
from jax import lax
from jax.experimental import pallas as pl
from jax.experimental.pallas import tpu as pltpu
from jax.sharding import PartitionSpec as P

STEPS = 4
RAD = 4
NOFF = 9
MESH = pl.DeviceIdType.MESH

second_w = (-205.0 / 72.0, 8.0 / 5.0, -1.0 / 5.0, 8.0 / 315.0, -1.0 / 560.0)
first_w = (4.0 / 5.0, -1.0 / 5.0, 4.0 / 105.0, -1.0 / 280.0)
SECOND_SCALE = 5040.0
FIRST_SCALE = 840.0
second_int = (0, 8064, -1008, 128, -9)
first_int = (672, -168, 32, -3)


def band(size, weights, odd):
    out = np.zeros((size, size), np.float32)
    for k, w in weights:
        out += w * np.eye(size, k=-k) + (-w if odd else w) * np.eye(size, k=k)
    return out


def depth_weights(nz):
    dzz = band(nz, [(k, second_int[k]) for k in range(1, 5)], False)
    dz = band(nz, [(k + 1, first_int[k]) for k in range(4)], True)
    return np.concatenate([dzz, dz], 1).astype(ml_dtypes.bfloat16)


def row_weights(ny, planes):
    dyy = band(ny, [(k, second_int[k]) for k in range(1, 5)], False)
    return np.kron(np.eye(planes), dyy).astype(ml_dtypes.bfloat16)


def split(value):
    high = value.astype(jnp.bfloat16)
    return high, (value - high.astype(jnp.float32)).astype(jnp.bfloat16)


def dot(a, b):
    return jnp.dot(a, b, preferred_element_type=jnp.float32)


def wave_kernel(
    count, sp, sc, rp, rc, ch_in, cv_in, cm_in, wz_in, wy_in, snaps,
    wave, dz, base, ch, cv, cm, wz, wy, load_sem, send_sem, recv_sem, out_sem, last_sem,
):
    bx, ny, nz = ch.shape
    rows = RAD * ny
    me = lax.axis_index("blk")
    outer = lax.rem(me, 2)
    inner = 1 - outer

    def beside(side):
        return me - 1 + 2 * side

    def there(side):
        return (beside(side) >= 0) & (beside(side) < count)

    loads = []
    for f, (prev, cur) in enumerate(((sp, sc), (rp, rc))):
        loads.append((prev.at[0], wave.at[0, f, pl.ds(RAD, bx)]))
        loads.append((cur.at[0], wave.at[1, f, pl.ds(RAD, bx)]))
    loads += [(ch_in.at[0], ch), (cv_in.at[0], cv), (cm_in.at[0], cm), (wz_in, wz), (wy_in, wy)]
    loads = [pltpu.make_async_copy(a, b, load_sem.at[j]) for j, (a, b) in enumerate(loads)]
    for load in loads:
        load.start()

    barrier = pltpu.get_barrier_semaphore()
    for side in (0, 1):
        @pl.when(there(side))
        def _():
            pl.semaphore_signal(
                barrier, inc=1, device_id={"blk": beside(side)}, device_id_type=MESH
            )
    peers = jnp.where(there(0), 1, 0) + jnp.where(there(1), 1, 0)
    pl.semaphore_wait(barrier, peers)

    def copy(level, f, way, to, src=None):
        if src is None:
            src = wave.at[level, f, pl.ds(RAD + (bx - RAD) * way, RAD)]
        return pltpu.make_async_remote_copy(
            src_ref=src,
            dst_ref=wave.at[level, f, pl.ds((RAD + bx) * (1 - way), RAD)],
            send_sem=send_sem.at[level, f, way],
            recv_sem=recv_sem.at[level, f, way],
            device_id={"blk": beside(to)},
            device_id_type=MESH,
        )

    def first_copy(f, way):
        return copy(1, f, way, way, (sc, rc)[f].at[0, pl.ds((bx - RAD) * way, RAD)])

    for way in (outer, inner):
        for f in (0, 1):
            @pl.when(there(way))
            def _():
                first_copy(f, way).start()

    for side in (0, 1):
        @pl.when(jnp.logical_not(there(side)))
        def _():
            def clear(level, carry):
                for f in (0, 1):
                    wave[level, f, pl.ds((RAD + bx) * side, RAD)] = jnp.zeros(
                        (RAD, ny, nz), jnp.float32
                    )
                return carry

            lax.fori_loop(1, STEPS + 2, clear, 0)

    def arrive(level, f, side):
        @pl.when(there(side))
        def _():
            copy(level, f, 1 - side, side).wait_recv()

    def local(level, f):
        def group(g, carry):
            own = pl.ds(RAD * g, RAD)
            at = pl.ds(RAD + RAD * g, RAD)
            now = wave[level, f, at]
            high, low = split(now.reshape(rows, nz))
            both = dot(high, wz[...]) + dot(low, wz[...])
            side = dot(wy[...], high) + dot(wy[...], low)
            dz[f, at] = both[:, nz:].reshape(RAD, ny, nz)
            dzz = both[:, :nz].reshape(RAD, ny, nz) * (1.0 / SECOND_SCALE) + second_w[0] * now
            dyy = side.reshape(RAD, ny, nz) * (1.0 / SECOND_SCALE) + 2.0 * second_w[0] * now
            base[f, own] = (
                2.0 * now - wave[level - 1, f, at] + ch[own] * dyy + cv[own] * dzz
            )
            return carry

        lax.fori_loop(0, bx // RAD, group, 0)

    def rim(level, f, side):
        at = pl.ds((RAD + bx) * side, RAD)
        high, low = split(wave[level, f, at].reshape(rows, nz))
        weights = wz[:, nz:]
        dz[f, at] = (dot(high, weights) + dot(low, weights)).reshape(RAD, ny, nz)

    def update(level, f, side):
        half = ny // 2

        def plane(j, carry):
            own = (bx - RAD) * side + j
            x = own + RAD
            for r in (0, half):
                at = pl.ds(r, half)
                flat, cross = None, None
                for k in range(1, RAD + 1):
                    a = second_w[k] * (wave[level, f, x + k, at] + wave[level, f, x - k, at])
                    b = (first_w[k - 1] / FIRST_SCALE) * (dz[f, x + k, at] - dz[f, x - k, at])
                    flat = a if flat is None else flat + a
                    cross = b if cross is None else cross + b
                wave[level + 1, f, x, at] = (
                    base[f, own, at] + ch[own, at] * flat + cm[own, at] * cross
                )
            return carry

        lax.fori_loop(0, RAD, plane, 0)

    for load in loads:
        load.wait()
    for f in (0, 1):
        local(1, f)

    mid = [pltpu.make_async_copy(wave.at[3, f], snaps.at[0, f], out_sem.at[f]) for f in (0, 1)]

    def step(level, carry):
        for f in (0, 1):
            for side in (outer, inner):
                arrive(level, f, side)
                rim(level, f, side)
                update(level, f, side)

                @pl.when(there(side))
                def _():
                    copy(level + 1, f, side, side).start()

            @pl.when(level < STEPS)
            def _():
                local(level + 1, f)

            @pl.when(level == 3)
            def _():
                mid[f].start()
        return carry

    lax.fori_loop(1, STEPS + 1, step, 0)

    last = STEPS + 1
    done = []
    for f in (0, 1):
        own = pl.ds(RAD, bx)
        done.append(
            pltpu.make_async_copy(wave.at[last, f, own], snaps.at[1, f, own], last_sem.at[f, 2])
        )
        done[-1].start()
    for f in (0, 1):
        for j, side in enumerate((inner, outer)):
            arrive(last, f, side)
            at = pl.ds((RAD + bx) * side, RAD)
            done.append(
                pltpu.make_async_copy(wave.at[last, f, at], snaps.at[1, f, at], last_sem.at[f, j])
            )
            done[-1].start()
    for item in mid + done:
        item.wait()
    for way in (0, 1):
        @pl.when(there(way))
        def _():
            for f in (0, 1):
                first_copy(f, way).wait_send()

            def sent(level, carry):
                for f in (0, 1):
                    copy(level, f, way, way).wait_send()
                return carry

            lax.fori_loop(2, STEPS + 2, sent, 0)


def image_kernel(offsets, live, snaps, image_in, image_out, source_last, receiver_last, mute):
    slot = pl.program_id(0)
    bx, ny, nz = mute.shape

    @pl.when(slot == 0)
    def _():
        row_ids = lax.broadcasted_iota(jnp.int32, (ny, ny), 0)
        diagonal = row_ids == lax.broadcasted_iota(jnp.int32, (ny, ny), 1)
        depth_ids = lax.broadcasted_iota(jnp.int32, (ny, nz), 1).astype(jnp.float32)
        for x in range(bx):
            depths = live[0, pl.ds(x, 1), :].astype(jnp.float32)
            column = jnp.sum(jnp.where(diagonal, depths, 0.0), axis=1, keepdims=True)
            mute[x] = (depth_ids < column).astype(jnp.float32)
        source_last[0] = snaps[1, 0, pl.ds(RAD, bx)]
        receiver_last[0] = snaps[1, 1, pl.ds(RAD, bx)]

    shift = offsets[slot] - RAD

    def plane(x, carry):
        left, right = RAD + x - shift, RAD + x + shift
        image_out[0, 0, x] = image_in[0, 0, x] + mute[x] * (
            snaps[0, 0, left] * snaps[0, 1, right] + snaps[1, 0, left] * snaps[1, 1, right]
        )
        return carry

    lax.fori_loop(0, bx, plane, 0)


def per_device(
    count,
    source_prev,
    source_cur,
    receiver_prev,
    receiver_cur,
    coef_horiz,
    coef_vert,
    coef_mixed,
    live_depth,
    offsets,
    image_in,
):
    _, bx, ny, nz = source_cur.shape
    f32 = jnp.float32
    slab = pltpu.VMEM((bx, ny, nz), f32)
    wz = jnp.asarray(depth_weights(nz))
    wy = jnp.asarray(row_weights(ny, RAD))
    full = bx + 2 * RAD
    any_space = pl.BlockSpec(memory_space=pl.ANY)
    snaps = pl.pallas_call(
        functools.partial(wave_kernel, count),
        out_shape=jax.ShapeDtypeStruct((2, 2, full, ny, nz), f32),
        in_specs=[any_space] * 9,
        out_specs=any_space,
        scratch_shapes=[
            pltpu.VMEM((STEPS + 2, 2, full, ny, nz), f32),
            pltpu.VMEM((2, full, ny, nz), f32),
            pltpu.VMEM((2, bx, ny, nz), f32),
            slab,
            slab,
            slab,
            pltpu.VMEM(wz.shape, jnp.bfloat16),
            pltpu.VMEM(wy.shape, jnp.bfloat16),
            pltpu.SemaphoreType.DMA((9,)),
            pltpu.SemaphoreType.DMA((STEPS + 2, 2, 2)),
            pltpu.SemaphoreType.DMA((STEPS + 2, 2, 2)),
            pltpu.SemaphoreType.DMA((2,)),
            pltpu.SemaphoreType.DMA((2, 3)),
        ],
        compiler_params=pltpu.CompilerParams(
            collective_id=0, has_side_effects=True, vmem_limit_bytes=40 * 2**20
        ),
        name="wave_steps",
    )(
        source_prev, source_cur, receiver_prev, receiver_cur,
        coef_horiz, coef_vert, coef_mixed, wz, wy,
    )
    slot_spec = pl.BlockSpec((1, 1, bx, ny, nz), lambda k, off: (k, 0, 0, 0, 0))
    last_spec = pl.BlockSpec((1, bx, ny, nz), lambda k, off: (0, 0, 0, 0))
    return pl.pallas_call(
        image_kernel,
        grid_spec=pltpu.PrefetchScalarGridSpec(
            num_scalar_prefetch=1,
            grid=(NOFF,),
            in_specs=[
                pl.BlockSpec((1, bx, ny), lambda k, off: (0, 0, 0)),
                pl.BlockSpec((2, 2, full, ny, nz), lambda k, off: (0, 0, 0, 0, 0)),
                slot_spec,
            ],
            out_specs=[slot_spec, last_spec, last_spec],
            scratch_shapes=[slab],
        ),
        out_shape=[
            jax.ShapeDtypeStruct(image_in.shape, f32),
            jax.ShapeDtypeStruct(source_cur.shape, f32),
            jax.ShapeDtypeStruct(receiver_cur.shape, f32),
        ],
        compiler_params=pltpu.CompilerParams(vmem_limit_bytes=40 * 2**20),
        name="image_terms",
    )(offsets, live_depth, snaps, image_in)


def solution(mesh):
    in_specs = (
        P(("shots", "blk"), None, None, None),
        P(("shots", "blk"), None, None, None),
        P(("shots", "blk"), None, None, None),
        P(("shots", "blk"), None, None, None),
        P("blk", None, None, None),
        P("blk", None, None, None),
        P("blk", None, None, None),
        P("blk", None, None),
        P(),
        P(None, ("shots", "blk"), None, None, None),
    )
    out_specs = (
        P(None, ("shots", "blk"), None, None, None),
        P(("shots", "blk"), None, None, None),
        P(("shots", "blk"), None, None, None),
    )
    return jax.shard_map(
        functools.partial(per_device, mesh.shape["blk"]),
        mesh=mesh,
        in_specs=in_specs,
        out_specs=out_specs,
        check_vma=False,
    )
```

time: 129 us -> 78.7 us (0.61)
  Pallas kernels: 0 us -> 67.2 us
  starting transfers between devices: 53.7 us -> 0 us
  other arithmetic: 41.7 us -> 0 us
  between operations: 24.2 us -> 0.69 us
  local copies, waits for them, and re-layouts: 3.98 us -> 9.58 us
  waiting for transfers between devices: 3.47 us -> 0 us
    pallas_call x0 -> x2, Pallas kernels: none -> 67.2 us  [the longest x1 61.1 us: per_device(): pl.pallas_call(functools.partial(wave_kernel, count), out_shape=jax.Shape...]
    ppermute x18 -> x0, starting transfers between devices: 53.7 us -> none  [from_behind(): lax.ppermute(value, axis, [(source, source + steps) for source in range(f...]
    add x15 -> x0, other arithmetic: 32.5 us -> none  [the longest x8 18.2 us: stencil(): deriv_z + first_w[k - 1] * (padded[:, 4:4 + count_y, 4 + k:4 + k + depth]...]
    unnamed x26 -> x24, local copies, waits for them, and re-layouts: 1.54 us -> 9.58 us
    another operation x5 -> x0, other arithmetic: 5.01 us -> none  [the longest x3 4.64 us: per_device(): snap_pad = snap_rims(jnp.stack([source_cur, receiver_cur]))]
    ppermute x18 -> x0, waiting for transfers between devices: 3.47 us -> none  [from_behind(): lax.ppermute(value, axis, [(source, source + steps) for source in range(f...]
    concatenate x9 -> x0, other arithmetic: 2.38 us -> none  [the longest x1 1.41 us: snap_rims(): return jnp.concatenate([from_below, snaps, from_above], 1)]
    slice x10 -> x0, local copies, waits for them, and re-layouts: 2.22 us -> none  [the longest x8 1.41 us: wave_rims(): lax.slice_in_dim(field, 0, RAD, axis=xdim)]
  transfers between devices with their start and end apart: 18 -> 0, of which waited for: 1 -> 0; matrix products, arithmetic and copies ran while one was open for 23% -> 0% of each run, Pallas kernels for 0% -> 0%
where the time goes in v1:
time: 78.7 us; the launch traced here: 77.5 us
  Pallas kernels  67.2 us (85%)
  local copies, waits for them, and re-layouts  9.58 us (12%)
    pallas_call x1, Pallas kernels, per_device(): pl.pallas_call(functools.partial(wave_kernel, count), out_shape=jax.Shape...  61.1 us
    unnamed x24, local copies, waits for them, and re-layouts  9.58 us
    pallas_call x1, Pallas kernels, per_device(): pl.pallas_call(image_kernel, grid_spec=pltpu.PrefetchScalarGridSpec(num_s...  6.1 us

profile of v1, /device:TPU:9, one launch (start us, length us, event | category | flops | bytes accessed | tf_op | source)
XLA Modules:
  0.0 77.5 jit_solution(8904384259320280388)
XLA Ops:
  0.6 0.0 copy-start
  0.6 0.0 copy-start.1
  0.7 1.2 %copy-done.1 = f32[1,8,64,256]{3,2,1,0:T(8,128)S(1)} copy-done((f32[1,8,64,256]{3,2,1,0:T(8,128)S(1)}, f32[1,8,64,256]{3,2,1,0:T(8,128)}, u32[]{:S(2)}) %copy-start.1) | copy-done | bytes 524312
  1.8 0.0 copy-start.2
  1.8 1.3 %copy-done.2 = f32[1,8,64,256]{3,2,1,0:T(8,128)S(1)} copy-done((f32[1,8,64,256]{3,2,1,0:T(8,128)S(1)}, f32[1,8,64,256]{3,2,1,0:T(8,128)}, u32[]{:S(2)}) %copy-start.2) | copy-done | bytes 524312
  3.2 0.0 copy-start.3
  3.2 1.0 %copy-done.3 = f32[1,8,64,256]{3,2,1,0:T(8,128)S(1)} copy-done((f32[1,8,64,256]{3,2,1,0:T(8,128)S(1)}, f32[1,8,64,256]{3,2,1,0:T(8,128)}, u32[]{:S(2)}) %copy-start.3) | copy-done | bytes 524312
  4.2 0.0 copy-start.4
  4.2 1.0 %copy-done.4 = f32[1,8,64,256]{3,2,1,0:T(8,128)S(1)} copy-done((f32[1,8,64,256]{3,2,1,0:T(8,128)S(1)}, f32[1,8,64,256]{3,2,1,0:T(8,128)}, u32[]{:S(2)}) %copy-start.4) | copy-done | bytes 524312
  5.2 0.0 copy-start.5
  5.3 1.0 %copy-done.5 = f32[1,8,64,256]{3,2,1,0:T(8,128)S(1)} copy-done((f32[1,8,64,256]{3,2,1,0:T(8,128)S(1)}, f32[1,8,64,256]{3,2,1,0:T(8,128)}, u32[]{:S(2)}) %copy-start.5) | copy-done | bytes 524312
  6.3 0.0 copy-start.6
  6.3 1.0 %copy-done.6 = f32[1,8,64,256]{3,2,1,0:T(8,128)S(1)} copy-done((f32[1,8,64,256]{3,2,1,0:T(8,128)S(1)}, f32[1,8,64,256]{3,2,1,0:T(8,128)}, u32[]{:S(2)}) %copy-start.6) | copy-done | bytes 524312
  7.3 0.0 copy-start.7
  7.3 1.0 %copy-done.7 = f32[1,8,64,256]{3,2,1,0:T(8,128)S(1)} copy-done((f32[1,8,64,256]{3,2,1,0:T(8,128)S(1)}, f32[1,8,64,256]{3,2,1,0:T(8,128)}, u32[]{:S(2)}) %copy-start.7) | copy-done | bytes 524312
  8.4 0.0 copy-start.8
  8.4 0.9 %copy-done.8 = bf16[256,512]{1,0:T(8,128)(2,1)S(1)} copy-done((bf16[256,512]{1,0:T(8,128)(2,1)S(1)}, bf16[256,512]{1,0:T(8,128)(2,1)}, u32[]{:S(2)}) %copy-start.8) | copy-done | bytes 262168
  9.3 0.0 copy-start.9
  9.3 0.9 %copy-done.9 = bf16[256,256]{1,0:T(8,128)(2,1)S(1)} copy-done((bf16[256,256]{1,0:T(8,128)(2,1)S(1)}, bf16[256,256]{1,0:T(8,128)(2,1)}, u32[]{:S(2)}) %copy-start.9) | copy-done | bytes 131096
  10.2 0.0 copy-start.10
  10.2 0.0 copy-start.11
  10.2 61.1 %wave_steps.1.snaps = f32[2,2,16,64,256]{4,3,2,1,0:T(8,128)S(1)} custom-call(f32[1,8,64,256]{3,2,1,0:T(8,128)S(1)} %copy-done.1, f32[1,8,64,256]{3,2,1,0:T(8,128)S(1)} %copy-done.2, f32[1,8,64,256]{3,2,1,0:T(8,128)S(1)} %copy-done.3, f32[1,8,64,256]{3,2,1,0:T(8,128)S(1)} %copy-done.4, f32[1,8,64,256]{3,2,1,0:T(8,128)S(1)} %copy-done.5, ...), custom_call_target="tpu_custom_call" | custom-call | tf_op jit(solution)/shard_map/wave_steps/pallas_call | solution.py:279
  71.3 0.0 copy-done
  71.3 0.0 copy-done.10
  71.3 0.0 copy-done.11
  71.4 6.1 %image_terms.1 = (f32[9,1,8,64,256]{4,3,2,1,0:T(8,128)}, f32[1,8,64,256]{3,2,1,0:T(8,128)}, f32[1,8,64,256]{3,2,1,0:T(8,128)}) custom-call(s32[9]{0:T(128)S(1)} %copy-done.11, s32[1,8,64]{2,1,0:T(8,128)S(1)} %copy-done.10, f32[2,2,16,64,256]{4,3,2,1,0:T(8,128)S(1)} %wave_steps.1.snaps, f32[9,1,8,64,256]{4,3,2,1,0:T(8,128)S(1)} %copy-done), custom_call_target="tpu_custom_call" | custom-call | tf_op jit(solution)/shard_map/image_terms/pallas_call | solution.py:309
Async XLA Ops:
  0.6 70.7 %copy-start = (f32[9,1,8,64,256]{4,3,2,1,0:T(8,128)S(1)}, f32[9,1,8,64,256]{4,3,2,1,0:T(8,128)}, u32[]{:S(2)}) copy-start(f32[9,1,8,64,256]{4,3,2,1,0:T(8,128)} %image_in.1) | copy-start | bytes 14155780
  0.6 1.2 %copy-start.1 = (f32[1,8,64,256]{3,2,1,0:T(8,128)S(1)}, f32[1,8,64,256]{3,2,1,0:T(8,128)}, u32[]{:S(2)}) copy-start(f32[1,8,64,256]{3,2,1,0:T(8,128)} %sp.1) | copy-start | bytes 1572868
  1.8 1.3 %copy-start.2 = (f32[1,8,64,256]{3,2,1,0:T(8,128)S(1)}, f32[1,8,64,256]{3,2,1,0:T(8,128)}, u32[]{:S(2)}) copy-start(f32[1,8,64,256]{3,2,1,0:T(8,128)} %sc.1) | copy-start | bytes 1572868
  3.2 1.0 %copy-start.3 = (f32[1,8,64,256]{3,2,1,0:T(8,128)S(1)}, f32[1,8,64,256]{3,2,1,0:T(8,128)}, u32[]{:S(2)}) copy-start(f32[1,8,64,256]{3,2,1,0:T(8,128)} %rp.1) | copy-start | bytes 1572868
  4.2 1.0 %copy-start.4 = (f32[1,8,64,256]{3,2,1,0:T(8,128)S(1)}, f32[1,8,64,256]{3,2,1,0:T(8,128)}, u32[]{:S(2)}) copy-start(f32[1,8,64,256]{3,2,1,0:T(8,128)} %rc.1) | copy-start | bytes 1572868
  5.2 1.0 %copy-start.5 = (f32[1,8,64,256]{3,2,1,0:T(8,128)S(1)}, f32[1,8,64,256]{3,2,1,0:T(8,128)}, u32[]{:S(2)}) copy-start(f32[1,8,64,256]{3,2,1,0:T(8,128)} %ch_in.1) | copy-start | bytes 1572868
  6.3 1.0 %copy-start.6 = (f32[1,8,64,256]{3,2,1,0:T(8,128)S(1)}, f32[1,8,64,256]{3,2,1,0:T(8,128)}, u32[]{:S(2)}) copy-start(f32[1,8,64,256]{3,2,1,0:T(8,128)} %cv_in.1) | copy-start | bytes 1572868
  7.3 1.0 %copy-start.7 = (f32[1,8,64,256]{3,2,1,0:T(8,128)S(1)}, f32[1,8,64,256]{3,2,1,0:T(8,128)}, u32[]{:S(2)}) copy-start(f32[1,8,64,256]{3,2,1,0:T(8,128)} %cm_in.1) | copy-start | bytes 1572868
  8.4 0.9 %copy-start.8 = (bf16[256,512]{1,0:T(8,128)(2,1)S(1)}, bf16[256,512]{1,0:T(8,128)(2,1)}, u32[]{:S(2)}) copy-start(bf16[256,512]{1,0:T(8,128)(2,1)} %constant.4.clone.wz_in) | copy-start | bytes 786436
  9.3 0.9 %copy-start.9 = (bf16[256,256]{1,0:T(8,128)(2,1)S(1)}, bf16[256,256]{1,0:T(8,128)(2,1)}, u32[]{:S(2)}) copy-start(bf16[256,256]{1,0:T(8,128)(2,1)} %constant.5.clone.wy_in) | copy-start | bytes 393220
  10.2 61.1 %copy-start.10 = (s32[1,8,64]{2,1,0:T(8,128)S(1)}, s32[1,8,64]{2,1,0:T(8,128)}, u32[]{:S(2)}) copy-start(s32[1,8,64]{2,1,0:T(8,128)} %live.1) | copy-start | bytes 6148
  10.2 61.1 %copy-start.11 = (s32[9]{0:T(128)S(1)}, s32[9]{0:T(128)}, u32[]{:S(2)}) copy-start(s32[9]{0:T(128)} %offsets.1) | copy-start | bytes 112

commit v2 on v1

--- a/solution.py
+++ b/solution.py
@@ -2,8 +2,6 @@
 
 import jax
 import jax.numpy as jnp
-import ml_dtypes
-import numpy as np
 from jax import lax
 from jax.experimental import pallas as pl
 from jax.experimental.pallas import tpu as pltpu
@@ -22,22 +20,16 @@
 first_int = (672, -168, 32, -3)
 
 
-def band(size, weights, odd):
-    out = np.zeros((size, size), np.float32)
+def band(size, weights, odd, block):
+    row = lax.broadcasted_iota(jnp.int32, (size, size), 0)
+    col = lax.broadcasted_iota(jnp.int32, (size, size), 1)
+    out = jnp.zeros((size, size), jnp.float32)
     for k, w in weights:
-        out += w * np.eye(size, k=-k) + (-w if odd else w) * np.eye(size, k=k)
-    return out
-
-
-def depth_weights(nz):
-    dzz = band(nz, [(k, second_int[k]) for k in range(1, 5)], False)
-    dz = band(nz, [(k + 1, first_int[k]) for k in range(4)], True)
-    return np.concatenate([dzz, dz], 1).astype(ml_dtypes.bfloat16)
-
-
-def row_weights(ny, planes):
-    dyy = band(ny, [(k, second_int[k]) for k in range(1, 5)], False)
-    return np.kron(np.eye(planes), dyy).astype(ml_dtypes.bfloat16)
+        out = jnp.where(row - col == k, float(w), out)
+        out = jnp.where(col - row == k, float(-w if odd else w), out)
+    for edge in range(block, size, block):
+        out = jnp.where((row < edge) == (col < edge), out, 0.0)
+    return out.astype(jnp.bfloat16)
 
 
 def split(value):
@@ -50,8 +42,10 @@
 
 
 def wave_kernel(
-    count, sp, sc, rp, rc, ch_in, cv_in, cm_in, wz_in, wy_in, snaps,
-    wave, dz, base, ch, cv, cm, wz, wy, load_sem, send_sem, recv_sem, out_sem, last_sem,
+    count, sp, sc, rp, rc, ch_in, cv_in, cm_in, image_in, live, offsets,
+    snaps, image_mid, mute_out,
+    wave, dz, base, ch, cv, cm, wz, wy, image, snap, mute,
+    load_sem, send_sem, recv_sem, out_sem, last_sem,
 ):
     bx, ny, nz = ch.shape
     rows = RAD * ny
@@ -69,7 +63,7 @@
     for f, (prev, cur) in enumerate(((sp, sc), (rp, rc))):
         loads.append((prev.at[0], wave.at[0, f, pl.ds(RAD, bx)]))
         loads.append((cur.at[0], wave.at[1, f, pl.ds(RAD, bx)]))
-    loads += [(ch_in.at[0], ch), (cv_in.at[0], cv), (cm_in.at[0], cm), (wz_in, wz), (wy_in, wy)]
+    loads += [(ch_in.at[0], ch), (cv_in.at[0], cv), (cm_in.at[0], cm)]
     loads = [pltpu.make_async_copy(a, b, load_sem.at[j]) for j, (a, b) in enumerate(loads)]
     for load in loads:
         load.start()
@@ -99,11 +93,13 @@
     def first_copy(f, way):
         return copy(1, f, way, way, (sc, rc)[f].at[0, pl.ds((bx - RAD) * way, RAD)])
 
-    for way in (outer, inner):
-        for f in (0, 1):
-            @pl.when(there(way))
-            def _():
-                first_copy(f, way).start()
+    for f, way in ((0, outer), (0, inner), (1, inner)):
+        @pl.when(there(way))
+        def _():
+            first_copy(f, way).start()
+
+    image_load = pltpu.make_async_copy(image_in.at[:, 0], image, out_sem.at[2])
+    image_load.start()
 
     for side in (0, 1):
         @pl.when(jnp.logical_not(there(side)))
@@ -167,12 +163,22 @@
 
         lax.fori_loop(0, RAD, plane, 0)
 
+    seconds = [(k, second_int[k]) for k in range(1, RAD + 1)]
+    firsts = [(k + 1, first_int[k]) for k in range(RAD)]
+    wz[:, :nz] = band(nz, seconds, False, nz)
+    wz[:, nz:] = band(nz, firsts, True, nz)
+    wy[...] = band(rows, seconds, False, ny)
     for load in loads:
         load.wait()
     for f in (0, 1):
         local(1, f)
 
-    mid = [pltpu.make_async_copy(wave.at[3, f], snaps.at[0, f], out_sem.at[f]) for f in (0, 1)]
+    @pl.when(there(outer))
+    def _():
+        first_copy(0, outer).wait_send()
+        first_copy(1, outer).start()
+
+    mid = [pltpu.make_async_copy(wave.at[3, f], snap.at[f], out_sem.at[f]) for f in (0, 1)]
 
     def step(level, carry):
         for f in (0, 1):
@@ -201,24 +207,53 @@
     for f in (0, 1):
         own = pl.ds(RAD, bx)
         done.append(
-            pltpu.make_async_copy(wave.at[last, f, own], snaps.at[1, f, own], last_sem.at[f, 2])
+            pltpu.make_async_copy(wave.at[last, f, own], snaps.at[f, own], last_sem.at[f, 2])
         )
         done[-1].start()
+
+    row_ids = lax.broadcasted_iota(jnp.int32, (ny, ny), 0)
+    diagonal = row_ids == lax.broadcasted_iota(jnp.int32, (ny, ny), 1)
+    depth_ids = lax.broadcasted_iota(jnp.int32, (ny, nz), 1).astype(jnp.float32)
+    for x in range(bx):
+        depths = live[0, pl.ds(x, 1), :].astype(jnp.float32)
+        column = jnp.sum(jnp.where(diagonal, depths, 0.0), axis=1, keepdims=True)
+        mute[x] = (depth_ids < column).astype(jnp.float32)
+    done.append(pltpu.make_async_copy(mute, mute_out, out_sem.at[3]))
+    done[-1].start()
+    for item in mid + [image_load]:
+        item.wait()
+
+    def slot_terms(slot, carry):
+        shift = offsets[slot] - RAD
+
+        def plane(x, inside):
+            image[slot, x] += mute[x] * snap[0, RAD + x - shift] * snap[1, RAD + x + shift]
+            return inside
+
+        return lax.fori_loop(0, bx, plane, carry)
+
+    lax.fori_loop(0, NOFF, slot_terms, 0)
+    done.append(pltpu.make_async_copy(image, image_mid, out_sem.at[2]))
+    done[-1].start()
+
     for f in (0, 1):
         for j, side in enumerate((inner, outer)):
             arrive(last, f, side)
             at = pl.ds((RAD + bx) * side, RAD)
             done.append(
-                pltpu.make_async_copy(wave.at[last, f, at], snaps.at[1, f, at], last_sem.at[f, j])
+                pltpu.make_async_copy(wave.at[last, f, at], snaps.at[f, at], last_sem.at[f, j])
             )
             done[-1].start()
-    for item in mid + done:
+    for item in done:
         item.wait()
     for way in (0, 1):
         @pl.when(there(way))
         def _():
-            for f in (0, 1):
-                first_copy(f, way).wait_send()
+            @pl.when(way == inner)
+            def _():
+                first_copy(0, way).wait_send()
+
+            first_copy(1, way).wait_send()
 
             def sent(level, carry):
                 for f in (0, 1):
@@ -228,32 +263,33 @@
             lax.fori_loop(2, STEPS + 2, sent, 0)
 
 
-def image_kernel(offsets, live, snaps, image_in, image_out, source_last, receiver_last, mute):
+def image_kernel(offsets, snaps, mute, image_in, image_out, source_last, receiver_last, sems):
     slot = pl.program_id(0)
-    bx, ny, nz = mute.shape
+    bx = mute.shape[0]
+    copies = [
+        pltpu.make_async_copy(snaps.at[f, pl.ds(RAD, bx)], last.at[0], sems.at[f])
+        for f, last in enumerate((source_last, receiver_last))
+    ]
 
     @pl.when(slot == 0)
     def _():
-        row_ids = lax.broadcasted_iota(jnp.int32, (ny, ny), 0)
-        diagonal = row_ids == lax.broadcasted_iota(jnp.int32, (ny, ny), 1)
-        depth_ids = lax.broadcasted_iota(jnp.int32, (ny, nz), 1).astype(jnp.float32)
-        for x in range(bx):
-            depths = live[0, pl.ds(x, 1), :].astype(jnp.float32)
-            column = jnp.sum(jnp.where(diagonal, depths, 0.0), axis=1, keepdims=True)
-            mute[x] = (depth_ids < column).astype(jnp.float32)
-        source_last[0] = snaps[1, 0, pl.ds(RAD, bx)]
-        receiver_last[0] = snaps[1, 1, pl.ds(RAD, bx)]
+        for item in copies:
+            item.start()
 
     shift = offsets[slot] - RAD
 
     def plane(x, carry):
-        left, right = RAD + x - shift, RAD + x + shift
-        image_out[0, 0, x] = image_in[0, 0, x] + mute[x] * (
-            snaps[0, 0, left] * snaps[0, 1, right] + snaps[1, 0, left] * snaps[1, 1, right]
+        image_out[0, 0, x] = image_in[0, x] + mute[x] * (
+            snaps[0, RAD + x - shift] * snaps[1, RAD + x + shift]
         )
         return carry
 
     lax.fori_loop(0, bx, plane, 0)
+
+    @pl.when(slot == pl.num_programs(0) - 1)
+    def _():
+        for item in copies:
+            item.wait()
 
 
 def per_device(
@@ -272,15 +308,19 @@
     _, bx, ny, nz = source_cur.shape
     f32 = jnp.float32
     slab = pltpu.VMEM((bx, ny, nz), f32)
-    wz = jnp.asarray(depth_weights(nz))
-    wy = jnp.asarray(row_weights(ny, RAD))
     full = bx + 2 * RAD
+    hbm = pl.BlockSpec(memory_space=pltpu.HBM)
     any_space = pl.BlockSpec(memory_space=pl.ANY)
-    snaps = pl.pallas_call(
+    snaps, image_mid, mute = pl.pallas_call(
         functools.partial(wave_kernel, count),
-        out_shape=jax.ShapeDtypeStruct((2, 2, full, ny, nz), f32),
-        in_specs=[any_space] * 9,
-        out_specs=any_space,
+        out_shape=[
+            jax.ShapeDtypeStruct((2, full, ny, nz), f32),
+            jax.ShapeDtypeStruct((NOFF, bx, ny, nz), f32),
+            jax.ShapeDtypeStruct((bx, ny, nz), f32),
+        ],
+        in_specs=[hbm] * 8
+        + [pl.BlockSpec(memory_space=pltpu.VMEM), pl.BlockSpec(memory_space=pltpu.SMEM)],
+        out_specs=[any_space] * 3,
         scratch_shapes=[
             pltpu.VMEM((STEPS + 2, 2, full, ny, nz), f32),
             pltpu.VMEM((2, full, ny, nz), f32),
@@ -288,45 +328,47 @@
             slab,
             slab,
             slab,
-            pltpu.VMEM(wz.shape, jnp.bfloat16),
-            pltpu.VMEM(wy.shape, jnp.bfloat16),
-            pltpu.SemaphoreType.DMA((9,)),
+            pltpu.VMEM((nz, 2 * nz), jnp.bfloat16),
+            pltpu.VMEM((RAD * ny, RAD * ny), jnp.bfloat16),
+            pltpu.VMEM((NOFF, bx, ny, nz), f32),
+            pltpu.VMEM((2, full, ny, nz), f32),
+            slab,
+            pltpu.SemaphoreType.DMA((7,)),
             pltpu.SemaphoreType.DMA((STEPS + 2, 2, 2)),
             pltpu.SemaphoreType.DMA((STEPS + 2, 2, 2)),
-            pltpu.SemaphoreType.DMA((2,)),
+            pltpu.SemaphoreType.DMA((4,)),
             pltpu.SemaphoreType.DMA((2, 3)),
         ],
         compiler_params=pltpu.CompilerParams(
-            collective_id=0, has_side_effects=True, vmem_limit_bytes=40 * 2**20
+            collective_id=0, has_side_effects=True, vmem_limit_bytes=58 * 2**20
         ),
         name="wave_steps",
     )(
         source_prev, source_cur, receiver_prev, receiver_cur,
-        coef_horiz, coef_vert, coef_mixed, wz, wy,
+        coef_horiz, coef_vert, coef_mixed, image_in, live_depth, offsets,
     )
     slot_spec = pl.BlockSpec((1, 1, bx, ny, nz), lambda k, off: (k, 0, 0, 0, 0))
-    last_spec = pl.BlockSpec((1, bx, ny, nz), lambda k, off: (0, 0, 0, 0))
     return pl.pallas_call(
         image_kernel,
         grid_spec=pltpu.PrefetchScalarGridSpec(
             num_scalar_prefetch=1,
             grid=(NOFF,),
             in_specs=[
-                pl.BlockSpec((1, bx, ny), lambda k, off: (0, 0, 0)),
-                pl.BlockSpec((2, 2, full, ny, nz), lambda k, off: (0, 0, 0, 0, 0)),
-                slot_spec,
+                pl.BlockSpec((2, full, ny, nz), lambda k, off: (0, 0, 0, 0)),
+                pl.BlockSpec((bx, ny, nz), lambda k, off: (0, 0, 0)),
+                pl.BlockSpec((1, bx, ny, nz), lambda k, off: (k, 0, 0, 0)),
             ],
-            out_specs=[slot_spec, last_spec, last_spec],
-            scratch_shapes=[slab],
+            out_specs=[slot_spec, any_space, any_space],
+            scratch_shapes=[pltpu.SemaphoreType.DMA((2,))],
         ),
         out_shape=[
             jax.ShapeDtypeStruct(image_in.shape, f32),
             jax.ShapeDtypeStruct(source_cur.shape, f32),
             jax.ShapeDtypeStruct(receiver_cur.shape, f32),
         ],
-        compiler_params=pltpu.CompilerParams(vmem_limit_bytes=40 * 2**20),
+        compiler_params=pltpu.CompilerParams(vmem_limit_bytes=58 * 2**20),
         name="image_terms",
-    )(offsets, live_depth, snaps, image_in)
+    )(offsets, snaps, mute, image_mid)
 
 
 def solution(mesh):

time: 78.7 us -> 78.5 us (level); the launches traced: 77.5 us -> 78.2 us
  Pallas kernels: 67.2 us -> 77.6 us
  local copies, waits for them, and re-layouts: 9.58 us -> 0 us
    unnamed x24 -> x0, local copies, waits for them, and re-layouts: 9.58 us -> none
    pallas_call x1, Pallas kernels: 61.1 us -> 68.2 us  [per_device(): pl.pallas_call(functools.partial(wave_kernel, count), out_shape=[jax.Shap...]
    pallas_call x1, Pallas kernels: 6.1 us -> 9.32 us  [per_device(): pl.pallas_call(image_kernel, grid_spec=pltpu.PrefetchScalarGridSpec(num_s...]
where the time goes in v2:
time: 78.5 us; the launch traced here: 78.2 us
  Pallas kernels  77.6 us (99%)
    pallas_call x1, Pallas kernels, per_device(): pl.pallas_call(functools.partial(wave_kernel, count), out_shape=[jax.Shap...  68.2 us
    pallas_call x1, Pallas kernels, per_device(): pl.pallas_call(image_kernel, grid_spec=pltpu.PrefetchScalarGridSpec(num_s...  9.32 us

profile of v2, /device:TPU:9, one launch (start us, length us, event | category | flops | bytes accessed | tf_op | source)
XLA Modules:
  0.0 78.2 jit_solution(8194776777708756548)
XLA Ops:
  0.6 68.2 %wave_steps.1 = (f32[2,16,64,256]{3,2,1,0:T(8,128)}, f32[9,8,64,256]{3,2,1,0:T(8,128)}, f32[8,64,256]{2,1,0:T(8,128)}) custom-call(f32[1,8,64,256]{3,2,1,0:T(8,128)} %sp.1, f32[1,8,64,256]{3,2,1,0:T(8,128)} %sc.1, f32[1,8,64,256]{3,2,1,0:T(8,128)} %rp.1, f32[1,8,64,256]{3,2,1,0:T(8,128)} %rc.1, f32[1,8,64,256]{3,2,1,0:T(8,128)} %ch_in.1, ...), custom_call_target="tpu_custom_call" | custom-call | tf_op jit(solution)/shard_map/wave_steps/pallas_call | solution.py:314
  68.9 9.3 %image_terms.1 = (f32[9,1,8,64,256]{4,3,2,1,0:T(8,128)}, f32[1,8,64,256]{3,2,1,0:T(8,128)}, f32[1,8,64,256]{3,2,1,0:T(8,128)}) custom-call(s32[9]{0:T(128)} %offsets.3, f32[2,16,64,256]{3,2,1,0:T(8,128)} %get-tuple-element.6.snaps, f32[8,64,256]{2,1,0:T(8,128)} %get-tuple-element.7.mute, f32[9,8,64,256]{3,2,1,0:T(8,128)} %get-tuple-element.8.image_in), custom_call_target="tpu_custom_call" | custom-call | tf_op jit(solution)/shard_map/image_terms/pallas_call | solution.py:351

commit v3 on v2

--- a/solution.py
+++ b/solution.py
@@ -93,7 +93,7 @@
     def first_copy(f, way):
         return copy(1, f, way, way, (sc, rc)[f].at[0, pl.ds((bx - RAD) * way, RAD)])
 
-    for f, way in ((0, outer), (0, inner), (1, inner)):
+    for f, way in ((0, outer), (1, outer), (0, inner), (1, inner)):
         @pl.when(there(way))
         def _():
             first_copy(f, way).start()
@@ -173,44 +173,6 @@
     for f in (0, 1):
         local(1, f)
 
-    @pl.when(there(outer))
-    def _():
-        first_copy(0, outer).wait_send()
-        first_copy(1, outer).start()
-
-    mid = [pltpu.make_async_copy(wave.at[3, f], snap.at[f], out_sem.at[f]) for f in (0, 1)]
-
-    def step(level, carry):
-        for f in (0, 1):
-            for side in (outer, inner):
-                arrive(level, f, side)
-                rim(level, f, side)
-                update(level, f, side)
-
-                @pl.when(there(side))
-                def _():
-                    copy(level + 1, f, side, side).start()
-
-            @pl.when(level < STEPS)
-            def _():
-                local(level + 1, f)
-
-            @pl.when(level == 3)
-            def _():
-                mid[f].start()
-        return carry
-
-    lax.fori_loop(1, STEPS + 1, step, 0)
-
-    last = STEPS + 1
-    done = []
-    for f in (0, 1):
-        own = pl.ds(RAD, bx)
-        done.append(
-            pltpu.make_async_copy(wave.at[last, f, own], snaps.at[f, own], last_sem.at[f, 2])
-        )
-        done[-1].start()
-
     row_ids = lax.broadcasted_iota(jnp.int32, (ny, ny), 0)
     diagonal = row_ids == lax.broadcasted_iota(jnp.int32, (ny, ny), 1)
     depth_ids = lax.broadcasted_iota(jnp.int32, (ny, nz), 1).astype(jnp.float32)
@@ -218,10 +180,11 @@
         depths = live[0, pl.ds(x, 1), :].astype(jnp.float32)
         column = jnp.sum(jnp.where(diagonal, depths, 0.0), axis=1, keepdims=True)
         mute[x] = (depth_ids < column).astype(jnp.float32)
-    done.append(pltpu.make_async_copy(mute, mute_out, out_sem.at[3]))
-    done[-1].start()
-    for item in mid + [image_load]:
-        item.wait()
+    mute_store = pltpu.make_async_copy(mute, mute_out, out_sem.at[3])
+    mute_store.start()
+    image_store = pltpu.make_async_copy(image, image_mid, out_sem.at[2])
+
+    mid = [pltpu.make_async_copy(wave.at[3, f], snap.at[f], out_sem.at[f]) for f in (0, 1)]
 
     def slot_terms(slot, carry):
         shift = offsets[slot] - RAD
@@ -232,9 +195,46 @@
 
         return lax.fori_loop(0, bx, plane, carry)
 
-    lax.fori_loop(0, NOFF, slot_terms, 0)
-    done.append(pltpu.make_async_copy(image, image_mid, out_sem.at[2]))
-    done[-1].start()
+    def step(level, carry):
+        for f in (0, 1):
+            for side in (outer, inner):
+                arrive(level, f, side)
+                rim(level, f, side)
+                update(level, f, side)
+
+                @pl.when(there(side))
+                def _():
+                    copy(level + 1, f, side, side).start()
+
+            @pl.when(level < STEPS)
+            def _():
+                local(level + 1, f)
+
+            @pl.when(level == 3)
+            def _():
+                mid[f].start()
+                if f == 1:
+                    for item in mid + [image_load]:
+                        item.wait()
+                    lax.fori_loop(0, NOFF // 2, slot_terms, 0)
+
+            if f == 0:
+                @pl.when(level == STEPS)
+                def _():
+                    lax.fori_loop(NOFF // 2, NOFF, slot_terms, 0)
+                    image_store.start()
+        return carry
+
+    lax.fori_loop(1, STEPS + 1, step, 0)
+
+    last = STEPS + 1
+    done = [mute_store, image_store]
+    for f in (0, 1):
+        own = pl.ds(RAD, bx)
+        done.append(
+            pltpu.make_async_copy(wave.at[last, f, own], snaps.at[f, own], last_sem.at[f, 2])
+        )
+        done[-1].start()
 
     for f in (0, 1):
         for j, side in enumerate((inner, outer)):
@@ -249,11 +249,8 @@
     for way in (0, 1):
         @pl.when(there(way))
         def _():
-            @pl.when(way == inner)
-            def _():
-                first_copy(0, way).wait_send()
-
-            first_copy(1, way).wait_send()
+            for f in (0, 1):
+                first_copy(f, way).wait_send()
 
             def sent(level, carry):
                 for f in (0, 1):
@@ -263,33 +260,53 @@
             lax.fori_loop(2, STEPS + 2, sent, 0)
 
 
-def image_kernel(offsets, snaps, mute, image_in, image_out, source_last, receiver_last, sems):
-    slot = pl.program_id(0)
+def image_kernel(
+    offsets, snaps_in, mute_in, image_in, image_out, source_last, receiver_last,
+    snaps, mute, image, load_sem, store_sem, side_sem,
+):
     bx = mute.shape[0]
-    copies = [
-        pltpu.make_async_copy(snaps.at[f, pl.ds(RAD, bx)], last.at[0], sems.at[f])
+    sides = [
+        pltpu.make_async_copy(snaps_in.at[0], snaps.at[0], side_sem.at[0]),
+        pltpu.make_async_copy(snaps_in.at[1], snaps.at[1], side_sem.at[1]),
+        pltpu.make_async_copy(mute_in, mute, side_sem.at[2]),
+    ]
+    for item in sides:
+        item.start()
+
+    def load(slot):
+        return pltpu.make_async_copy(image_in.at[slot], image.at[slot], load_sem.at[slot])
+
+    def store(slot):
+        return pltpu.make_async_copy(image.at[slot], image_out.at[slot, 0], store_sem.at[slot])
+
+    for slot in range(NOFF):
+        load(slot).start()
+    for item in sides:
+        item.wait()
+    lasts = [
+        pltpu.make_async_copy(snaps.at[f, pl.ds(RAD, bx)], last.at[0], side_sem.at[3 + f])
         for f, last in enumerate((source_last, receiver_last))
     ]
 
-    @pl.when(slot == 0)
-    def _():
-        for item in copies:
-            item.start()
-
-    shift = offsets[slot] - RAD
-
-    def plane(x, carry):
-        image_out[0, 0, x] = image_in[0, x] + mute[x] * (
-            snaps[0, RAD + x - shift] * snaps[1, RAD + x + shift]
-        )
+    def terms(slot, carry):
+        load(slot).wait()
+        shift = offsets[slot] - RAD
+
+        def plane(x, inside):
+            image[slot, x] += mute[x] * snaps[0, RAD + x - shift] * snaps[1, RAD + x + shift]
+            return inside
+
+        lax.fori_loop(0, bx, plane, 0)
+        store(slot).start()
         return carry
 
-    lax.fori_loop(0, bx, plane, 0)
-
-    @pl.when(slot == pl.num_programs(0) - 1)
-    def _():
-        for item in copies:
-            item.wait()
+    lax.fori_loop(0, NOFF, terms, 0)
+    for item in lasts:
+        item.start()
+    for slot in range(NOFF):
+        store(slot).wait()
+    for item in lasts:
+        item.wait()
 
 
 def per_device(
@@ -347,20 +364,18 @@
         source_prev, source_cur, receiver_prev, receiver_cur,
         coef_horiz, coef_vert, coef_mixed, image_in, live_depth, offsets,
     )
-    slot_spec = pl.BlockSpec((1, 1, bx, ny, nz), lambda k, off: (k, 0, 0, 0, 0))
     return pl.pallas_call(
         image_kernel,
-        grid_spec=pltpu.PrefetchScalarGridSpec(
-            num_scalar_prefetch=1,
-            grid=(NOFF,),
-            in_specs=[
-                pl.BlockSpec((2, full, ny, nz), lambda k, off: (0, 0, 0, 0)),
-                pl.BlockSpec((bx, ny, nz), lambda k, off: (0, 0, 0)),
-                pl.BlockSpec((1, bx, ny, nz), lambda k, off: (k, 0, 0, 0)),
-            ],
-            out_specs=[slot_spec, any_space, any_space],
-            scratch_shapes=[pltpu.SemaphoreType.DMA((2,))],
-        ),
+        in_specs=[pl.BlockSpec(memory_space=pltpu.SMEM)] + [hbm] * 3,
+        out_specs=[hbm] * 3,
+        scratch_shapes=[
+            pltpu.VMEM((2, full, ny, nz), f32),
+            slab,
+            pltpu.VMEM((NOFF, bx, ny, nz), f32),
+            pltpu.SemaphoreType.DMA((NOFF,)),
+            pltpu.SemaphoreType.DMA((NOFF,)),
+            pltpu.SemaphoreType.DMA((5,)),
+        ],
         out_shape=[
             jax.ShapeDtypeStruct(image_in.shape, f32),
             jax.ShapeDtypeStruct(source_cur.shape, f32),

time: 78.5 us -> 70.4 us (0.90)
  Pallas kernels: 77.6 us -> 68.8 us
    pallas_call x1, Pallas kernels: 68.2 us -> 62.3 us  [per_device(): pl.pallas_call(functools.partial(wave_kernel, count), out_shape=[jax.Shap...]
    pallas_call x1, Pallas kernels: 9.32 us -> 6.41 us  [per_device(): pl.pallas_call(image_kernel, in_specs=[pl.BlockSpec(memory_space=pltpu.SM...]
where the time goes in v3:
time: 70.4 us; the launch traced here: 69.4 us
  Pallas kernels  68.8 us (98%)
    pallas_call x1, Pallas kernels, per_device(): pl.pallas_call(functools.partial(wave_kernel, count), out_shape=[jax.Shap...  62.3 us
    pallas_call x1, Pallas kernels, per_device(): pl.pallas_call(image_kernel, in_specs=[pl.BlockSpec(memory_space=pltpu.SM...  6.41 us

profile of v3, /device:TPU:9, one launch (start us, length us, event | category | flops | bytes accessed | tf_op | source)
XLA Modules:
  0.0 69.4 jit_solution(16762340811708695583)
XLA Ops:
  0.6 62.3 %wave_steps.1 = (f32[2,16,64,256]{3,2,1,0:T(8,128)}, f32[9,8,64,256]{3,2,1,0:T(8,128)}, f32[8,64,256]{2,1,0:T(8,128)}) custom-call(f32[1,8,64,256]{3,2,1,0:T(8,128)} %sp.1, f32[1,8,64,256]{3,2,1,0:T(8,128)} %sc.1, f32[1,8,64,256]{3,2,1,0:T(8,128)} %rp.1, f32[1,8,64,256]{3,2,1,0:T(8,128)} %rc.1, f32[1,8,64,256]{3,2,1,0:T(8,128)} %ch_in.1, ...), custom_call_target="tpu_custom_call" | custom-call | tf_op jit(solution)/shard_map/wave_steps/pallas_call | solution.py:331
  63.0 6.4 %image_terms.1 = (f32[9,1,8,64,256]{4,3,2,1,0:T(8,128)}, f32[1,8,64,256]{3,2,1,0:T(8,128)}, f32[1,8,64,256]{3,2,1,0:T(8,128)}) custom-call(s32[9]{0:T(128)} %offsets.3, f32[2,16,64,256]{3,2,1,0:T(8,128)} %get-tuple-element.6.snaps_in, f32[8,64,256]{2,1,0:T(8,128)} %get-tuple-element.7.mute_in, f32[9,8,64,256]{3,2,1,0:T(8,128)} %get-tuple-element.8.image_in), custom_call_target="tpu_custom_call" | custom-call | tf_op jit(solution)/shard_map/image_terms/pallas_call | solution.py:367

commit v4 on v3

--- a/solution.py
+++ b/solution.py
@@ -161,7 +161,7 @@
                 )
             return carry
 
-        lax.fori_loop(0, RAD, plane, 0)
+        lax.fori_loop(0, RAD, plane, 0, unroll=2)
 
     seconds = [(k, second_int[k]) for k in range(1, RAD + 1)]
     firsts = [(k + 1, first_int[k]) for k in range(RAD)]
@@ -296,7 +296,7 @@
             image[slot, x] += mute[x] * snaps[0, RAD + x - shift] * snaps[1, RAD + x + shift]
             return inside
 
-        lax.fori_loop(0, bx, plane, 0)
+        lax.fori_loop(0, bx, plane, 0, unroll=True)
         store(slot).start()
         return carry
 

time: 70.4 us -> 70.4 us (level)
  no operation moved by 1% of the time
where the time goes in v4:
time: 70.4 us; the launch traced here: 69.3 us
  Pallas kernels  68.7 us (98%)
    pallas_call x1, Pallas kernels, per_device(): pl.pallas_call(functools.partial(wave_kernel, count), out_shape=[jax.Shap...  62.3 us
    pallas_call x1, Pallas kernels, per_device(): pl.pallas_call(image_kernel, in_specs=[pl.BlockSpec(memory_space=pltpu.SM...  6.37 us

profile of v4, /device:TPU:9, one launch (start us, length us, event | category | flops | bytes accessed | tf_op | source)
XLA Modules:
  0.0 69.3 jit_solution(11584184877066505612)
XLA Ops:
  0.6 62.3 %wave_steps.1 = (f32[2,16,64,256]{3,2,1,0:T(8,128)}, f32[9,8,64,256]{3,2,1,0:T(8,128)}, f32[8,64,256]{2,1,0:T(8,128)}) custom-call(f32[1,8,64,256]{3,2,1,0:T(8,128)} %sp.1, f32[1,8,64,256]{3,2,1,0:T(8,128)} %sc.1, f32[1,8,64,256]{3,2,1,0:T(8,128)} %rp.1, f32[1,8,64,256]{3,2,1,0:T(8,128)} %rc.1, f32[1,8,64,256]{3,2,1,0:T(8,128)} %ch_in.1, ...), custom_call_target="tpu_custom_call" | custom-call | tf_op jit(solution)/shard_map/wave_steps/pallas_call | solution.py:331
  63.0 6.4 %image_terms.1 = (f32[9,1,8,64,256]{4,3,2,1,0:T(8,128)}, f32[1,8,64,256]{3,2,1,0:T(8,128)}, f32[1,8,64,256]{3,2,1,0:T(8,128)}) custom-call(s32[9]{0:T(128)} %offsets.3, f32[2,16,64,256]{3,2,1,0:T(8,128)} %get-tuple-element.6.snaps_in, f32[8,64,256]{2,1,0:T(8,128)} %get-tuple-element.7.mute_in, f32[9,8,64,256]{3,2,1,0:T(8,128)} %get-tuple-element.8.image_in), custom_call_target="tpu_custom_call" | custom-call | tf_op jit(solution)/shard_map/image_terms/pallas_call | solution.py:367
